TPU v7x, 512 devices: a whole 4x8x8 slice. The times are simulated.
512 devices in a mesh: seq: 32 (over x_hi, z, core), exp: 16 (over y, x_lo).
Axes of the slice: x: 4 (x_hi: 2, x_lo: 2; x = x_hi * 2 + x_lo), y: 8, z: 8, core: 2. Of those that a mesh axis runs over, the one named last changes fastest.
Arguments:
- tokens: bfloat16 [262144, 1280], P(('seq', 'exp')), may hold values from -1024 to 1024
- slot_embed: bfloat16 [256, 1280], P('exp', 'seq'), may hold values from -2 to 2
- slot_outputs: bfloat16 [256, 1280], P('exp', 'seq'), may hold values from -6 to 6
- output_grad: bfloat16 [262144, 1280], P(('seq', 'exp')), may hold values from -2560 to 2560
- slot_input_grad: bfloat16 [256, 1280], P('exp', 'seq'), may hold values from -73728 to 73728
Outputs:
- token_grad: bfloat16 [262144, 1280], P(('seq', 'exp'))
- embed_grad: float32 [256, 1280], P('exp', 'seq')
- slot_output_grad: float32 [256, 1280], P('exp', 'seq')
All inputs are finite; a program needn't handle non-finite values.
Results may differ from a plain program's by a relative error of at most 0.0051.
Values may be sent and summed in bfloat16 or wider, within the bound.
No kernel may reach another device: no remote copies, remote signals or barrier semaphores. Data moves between devices by JAX's collectives and lax.ppermute only.
A program may use at most 64 MiB of HBM per device.

v0:
```python
import jax
import jax.numpy as jnp
from jax import lax
from jax.sharding import PartitionSpec as P


def contract_last(left, right):
    return lax.dot_general(
        left, right, (((1,), (1,)), ((), ())), preferred_element_type=jnp.float32
    )


def contract_first(left, right):
    return lax.dot_general(
        left, right, (((0,), (0,)), ((), ())), preferred_element_type=jnp.float32
    )


def per_device(tokens, slot_embed, slot_outputs, output_grad, slot_input_grad):
    pieces = (
        lax.all_gather(slot_embed, "seq", axis=1, tiled=True),
        lax.all_gather(slot_outputs, "seq", axis=1, tiled=True),
        lax.all_gather(slot_input_grad, "seq", axis=1, tiled=True),
    )
    embed_all, outputs_all, inputs_all = (
        lax.all_gather(pieces[0], "exp", axis=0, tiled=True),
        lax.all_gather(pieces[1], "exp", axis=0, tiled=True),
        lax.all_gather(pieces[2], "exp", axis=0, tiled=True),
    )
    logits = contract_last(tokens, embed_all)
    combine = jax.nn.softmax(logits, axis=1)
    dispatch_grad = contract_last(tokens, inputs_all)
    combine_grad = contract_last(output_grad, outputs_all)
    local_max = jnp.max(logits, axis=0)
    col_max = lax.pmax(local_max, ("seq", "exp"))
    raised = jnp.exp(logits - col_max[None, :])
    col_total = lax.psum(jnp.sum(raised, axis=0), ("seq", "exp"))
    dispatch = raised / col_total[None, :]
    column_term = lax.psum(jnp.sum(dispatch * dispatch_grad, axis=0), ("seq", "exp"))
    row_term = jnp.sum(combine * combine_grad, axis=1, keepdims=True)
    logit_grad = (
        combine * (combine_grad - row_term) + dispatch * (dispatch_grad - column_term[None, :])
    ).astype(jnp.bfloat16)
    dispatch_low = dispatch.astype(jnp.bfloat16)
    combine_low = combine.astype(jnp.bfloat16)
    outputs_part = contract_first(combine_low, output_grad)
    embed_part = contract_first(logit_grad, tokens)
    owned = lax.psum_scatter(
        jnp.stack([outputs_part, embed_part], axis=1), "exp", scatter_dimension=0, tiled=True
    )
    summed = lax.psum_scatter(owned, "seq", scatter_dimension=2, tiled=True)
    token_grad = (
        jnp.dot(logit_grad, embed_all, preferred_element_type=jnp.float32)
        + jnp.dot(dispatch_low, inputs_all, preferred_element_type=jnp.float32)
    ).astype(jnp.bfloat16)
    return (token_grad, summed[:, 1], summed[:, 0])


def solution(mesh):
    placed = (
        P(("seq", "exp"), None),
        P("exp", "seq"),
        P("exp", "seq"),
        P(("seq", "exp"), None),
        P("exp", "seq"),
    )
    return jax.shard_map(
        per_device,
        mesh=mesh,
        in_specs=placed,
        out_specs=(P(("seq", "exp"), None), P("exp", "seq"), P("exp", "seq")),
        check_vma=False,
    )
```

profile of v0, /device:TPU:1, one launch (start us, length us, event | category | flops | bytes accessed | tf_op | source)
XLA Modules:
  0.0 871.4 jit_solution(3574582479194960160)
XLA Ops:
  7.2 0.0 copy-start
  7.2 0.0 reduce-scatter.3.cloned.1.call-start
  7.2 49.9 %all-gather.2 = bf16[32,40,16]{1,2,0:T(8,128)(2,1)S(1)} all-gather(bf16[1,40,16]{1,2,0:T(8,128)(2,1)} %bitcast.46), channel_id=1, replica_groups=mesh['seq'=32,'exp'=16] {'seq'}, dimensions={0}, use_global_device_ids=true | all-gather | bytes 42240 | tf_op jit(solution)/shard_map/all_gather | solution.py:23
  57.2 0.2 reshape.17
  57.4 29.8 %all_gather.23 = bf16[256,1280]{1,0:T(8,128)(2,1)S(1)} all-gather(bf16[16,1280]{1,0:T(8,128)(2,1)S(1)} %bitcast.43), channel_id=1, replica_groups=mesh['seq'=32,'exp'=16] {'exp'}, dimensions={0}, use_global_device_ids=true | all-gather | bytes 696320 | tf_op jit(solution)/shard_map/all_gather | solution.py:28
  87.2 44.0 %all-gather = bf16[32,40,16]{1,2,0:T(8,128)(2,1)S(1)} all-gather(bf16[1,40,16]{1,2,0:T(8,128)(2,1)} %bitcast.47), channel_id=1, replica_groups=mesh['seq'=32,'exp'=16] {'seq'}, dimensions={0}, use_global_device_ids=true | all-gather | bytes 42240 | tf_op jit(solution)/shard_map/all_gather | solution.py:21
  131.2 0.2 reshape.13
  131.4 26.7 %all_gather.19 = bf16[256,1280]{1,0:T(8,128)(2,1)S(1)} all-gather(bf16[16,1280]{1,0:T(8,128)(2,1)S(1)} %bitcast.44), channel_id=1, replica_groups=mesh['seq'=32,'exp'=16] {'exp'}, dimensions={0}, use_global_device_ids=true | all-gather | bytes 696320 | tf_op jit(solution)/shard_map/all_gather | solution.py:26
  158.1 1.3 fusion.10
  159.5 0.6 fusion.9
  160.1 102.5 %pmax.7 = f32[256]{0:T(256)S(1)} all-reduce(f32[256]{0:T(256)S(1)} %get-tuple-element.8), channel_id=1, replica_groups=mesh['seq'=32,'exp'=16] {'seq','exp'}, use_global_device_ids=true, to_apply=%region_4.0 | all-reduce | flops 256 | bytes 2048 | tf_op jit(solution)/shard_map/pmax | solution.py:35
  262.6 0.2 fusion.2
  262.9 93.4 %psum.14 = f32[256]{0:T(256)S(1)} all-reduce(f32[256]{0:T(256)S(1)} %get-tuple-element.6), channel_id=1, replica_groups=mesh['seq'=32,'exp'=16] {'seq','exp'}, use_global_device_ids=true, to_apply=%region_6.0 | all-reduce | flops 256 | bytes 2048 | tf_op jit(solution)/shard_map/psum | solution.py:37
  356.3 39.9 %all-gather.1 = bf16[32,40,16]{1,2,0:T(8,128)(2,1)S(1)} all-gather(bf16[1,40,16]{1,2,0:T(8,128)(2,1)S(1)} %bitcast.48), channel_id=1, replica_groups=mesh['seq'=32,'exp'=16] {'seq'}, dimensions={0}, use_global_device_ids=true | all-gather | bytes 42240 | tf_op jit(solution)/shard_map/all_gather | solution.py:22
  396.2 0.2 reshape.15
  396.4 28.0 %all_gather.21 = bf16[256,1280]{1,0:T(8,128)(2,1)S(1)} all-gather(bf16[16,1280]{1,0:T(8,128)(2,1)S(1)} %bitcast.45), channel_id=1, replica_groups=mesh['seq'=32,'exp'=16] {'exp'}, dimensions={0}, use_global_device_ids=true | all-gather | bytes 696320 | tf_op jit(solution)/shard_map/all_gather | solution.py:27
  424.4 3.2 convolution_bitcast_fusion.1
  427.6 1.4 multiply_reduce_fusion.1
  429.0 99.6 %psum.15 = f32[256]{0:T(256)S(1)} all-reduce(f32[256]{0:T(256)S(1)} %get-tuple-element.4), channel_id=1, replica_groups=mesh['seq'=32,'exp'=16] {'seq','exp'}, use_global_device_ids=true, to_apply=%region_8.0 | all-reduce | flops 256 | bytes 2048 | tf_op jit(solution)/shard_map/psum | solution.py:39
  528.5 1.5 add_convert_fusion
  530.0 0.5 convolution_bitcast_fusion
  530.5 0.8 copy-done.2
  531.3 1.7 pad_maximum_fusion
  533.0 0.0 reduce-scatter.3.cloned.1.call-update
  533.0 0.0 all-reduce.3.cloned.1.call-start
  533.1 2.0 fusion.11
  535.1 62.4 %reduce-scatter.3.cloned.1.call-done = f32[16,2,1280]{2,0,1:T(8,128)} async-done(((f32[256,2,1280]{2,0,1:T(8,128)}), f32[16,2,1280]{2,0,1:T(8,128)}) %reduce-scatter.3.cloned.1.call-update) | async-done | bytes 163856 | tf_op jit(solution)/shard_map/reduce_scatter | solution.py:48
  597.5 0.0 all-reduce.3.cloned.1.call-update
  597.6 3.3 fusion
  600.9 1.3 dynamic-slice
  602.8 260.3 %all-reduce.3.cloned.1.call-done = f32[16,2,1280]{2,0,1:T(8,128)} async-done(((f32[16,2,1280]{2,0,1:T(8,128)}), f32[16,2,1280]{2,0,1:T(8,128)}) %all-reduce.3.cloned.1.call-update) | async-done | bytes 163856
  863.1 1.4 dynamic-slice_bitcast_fusion
  (11 shorter events, 0.1 us)
Async XLA Ops:
  7.2 151.0 %copy-start = (bf16[512,1280]{1,0:T(8,128)(2,1)S(1)}, bf16[512,1280]{1,0:T(8,128)(2,1)}, u32[]{:S(2)}) copy-start(bf16[512,1280]{1,0:T(8,128)(2,1)} %param.5) | copy-start | bytes 3932164
  7.2 590.4 %reduce-scatter.3.cloned.1.call-start = ((), (), s32[]{:S(2)}) async-start(), calls=%async_computation.1 | async-start | bytes 2785280 | tf_op jit(solution)/shard_map/reduce_scatter | solution.py:48
  159.5 196.8 %copy-start.3 = (bf16[16,40]{1,0:T(8,128)(2,1)S(1)}, bf16[16,40]{1,0:T(8,128)(2,1)}, u32[]{:S(2)}) copy-start(bf16[16,40]{1,0:T(8,128)(2,1)} %param.7) | copy-start | bytes 3844
  424.4 3.2 copy-start.1
  424.4 3.2 copy-start.4
  530.0 1.3 copy-start.2
  533.0 330.1 %all-reduce.3.cloned.1.call-start = ((), (), s32[]{:S(2)}) async-start(), calls=%async_computation.2 | async-start | bytes 327680
Sparse Core Ops, SparseCore 0:
  533.2 64.3 reduce-scatter.2
  600.4 262.6 all-reduce.2
where the time goes:
time: 872 us; the launch traced here: 871 us
  blocking collectives  514 us (59%)
  waiting for transfers between devices  323 us (37%)
  between operations  14.7 us (2%)
  matrix products  12.4 us (1%)
    unnamed x3, waiting for transfers between devices  260 us
    pmax x1, blocking collectives, per_device(): col_max = lax.pmax(local_max, ('seq', 'exp'))  103 us
    psum x1, blocking collectives, per_device(): lax.psum(jnp.sum(dispatch * dispatch_grad, axis=0), ('seq', 'exp'))  99.6 us
    psum x1, blocking collectives, per_device(): col_total = lax.psum(jnp.sum(raised, axis=0), ('seq', 'exp'))  93.4 us
    reduce_scatter x1, waiting for transfers between devices, per_device(): lax.psum_scatter(jnp.stack([outputs_part, embed_part], axis=1), 'exp', sc...  62.4 us
    all_gather x1, blocking collectives, per_device(): lax.all_gather(slot_input_grad, 'seq', axis=1, tiled=True)  49.9 us
    all_gather x1, blocking collectives, per_device(): lax.all_gather(slot_embed, 'seq', axis=1, tiled=True)  44 us
    all_gather x1, blocking collectives, per_device(): lax.all_gather(slot_outputs, 'seq', axis=1, tiled=True)  39.9 us
  transfers between devices with their start and end apart: 2, of which 2 were waited for; matrix products, arithmetic and copies ran while one was open for 1% of the time, Pallas kernels for 0%

commit v1 on v0

v1 whole, which is shorter than its diff:
```python
import jax
import jax.numpy as jnp
from jax import lax
from jax.sharding import Mesh, PartitionSpec as P

BF = jnp.bfloat16
F32 = jnp.float32
YZ = ("z", "core", "y")
X = ("xh", "xl")


def nt(a, b):
    return lax.dot_general(a, b, (((1,), (1,)), ((), ())), preferred_element_type=F32)


def nn(a, b):
    return lax.dot_general(a, b, (((1,), (0,)), ((), ())), preferred_element_type=F32)


def tn(a, b):
    return lax.dot_general(a, b, (((0,), (0,)), ((), ())), preferred_element_type=F32)


def low(x):
    return lax.reduce_precision(x, 8, 7)


def split3(x):
    a = low(x)
    b = low(x - a)
    return [a.astype(BF), b.astype(BF), (x - a - b).astype(BF)]


def pack(m, s, t):
    return jnp.stack(split3(m) + split3(s)[:2] + split3(t), axis=0)


def unpack(p):
    p = p.astype(F32)
    return p[0] + p[1] + p[2], p[3] + p[4], p[5] + p[6] + p[7]


def merge(m, s, t):
    top = jnp.max(m, axis=0)
    w = jnp.exp(m - top[None])
    ws = w * s
    total = jnp.sum(ws, axis=0)
    mean = jnp.sum(ws * t, axis=0) / total
    return top, total, mean, w, t - mean[None]


def merge_data(d, w, dt):
    d = d.astype(F32)
    w = w[:, :, None]
    dt = dt[:, :, None]
    o = jnp.sum(d[:, 0], 0)
    a = jnp.sum(d[:, 1], 0)
    b = jnp.sum(w * (d[:, 2] + dt * d[:, 3]), 0)
    c = jnp.sum(w * d[:, 3], 0)
    return jnp.stack([o, a, b, c], 0)


def swap(x):
    return lax.ppermute(x, "core", [(0, 1), (1, 0)])


def per_device(tokens, slot_embed, slot_outputs, output_grad, slot_input_grad):
    piece = jnp.stack([slot_embed, slot_outputs, slot_input_grad])
    piece = piece.reshape(3, 2, 8, 40).transpose(1, 0, 2, 3).reshape(1, 2, 1, 960)
    op = jnp.broadcast_to(piece, (8, 2, 8, 960)).reshape(128, 960)
    got = lax.all_to_all(op, YZ, 0, 0, tiled=True)
    got = got.reshape(8, 2, 8, 3, 8, 40).transpose(3, 4, 2, 0, 1, 5).reshape(192, 640)
    got = lax.all_to_all(jnp.broadcast_to(got[None], (4, 192, 640)), X, 0, 0, tiled=True)
    own = got
    sib = swap(got)
    full = jnp.stack([own, sib]).reshape(2, 2, 2, 3, 64, 640)
    full = full.transpose(3, 0, 2, 4, 1, 5).reshape(3, 256, 1280)
    embed_all, outputs_all, inputs_all = full[0], full[1], full[2]

    logits = nt(embed_all, tokens)
    dgrad = nt(inputs_all, tokens)
    cgrad = nt(outputs_all, output_grad)
    combine = jax.nn.softmax(logits, axis=0)
    row = jnp.sum(combine * cgrad, axis=0, keepdims=True)
    part = combine * (cgrad - row)
    m = jnp.max(logits, axis=1)
    e = jnp.exp(logits - m[:, None])
    s = jnp.sum(e, axis=1)
    t = jnp.sum(e * dgrad, axis=1) / s
    dc = dgrad - t[:, None]
    o = nn(combine.astype(BF), output_grad)
    a = nn(part.astype(BF), tokens)
    b = nn((e * dc).astype(BF), tokens)
    c = nn(e.astype(BF), tokens)
    data = jnp.stack([o, a, b, c]).astype(BF)

    st = pack(m, s, t)
    st2 = swap(st)
    st2 = jnp.concatenate([st2[:, 128:], st2[:, :128]], 1)
    d2 = swap(data[:, 128:])
    ms, ss, ts = unpack(jnp.stack([st, st2], 1))
    m1, s1, t1, w, dt = merge(ms, ss, ts)
    d = merge_data(jnp.stack([data[:, :128], d2]), w[:, :128], dt[:, :128]).astype(BF)

    d = d.reshape(4, 2, 64, 2, 640).transpose(3, 1, 0, 2, 4).reshape(4, 256, 640)
    st = jnp.pad(pack(m1, s1, t1), ((0, 8), (0, 384)))
    op = jnp.concatenate([d, jnp.broadcast_to(st[None], (4, 16, 640))], 1)
    got = lax.all_to_all(op, X, 0, 0, tiled=True)
    ms, ss, ts = unpack(got[:, 256:264, :256].transpose(1, 0, 2))
    m2, s2, t2, w, dt = merge(ms, ss, ts)
    xl = lax.axis_index("xl")
    wx = lax.dynamic_slice_in_dim(w[:, :128], xl * 64, 64, 1)
    dx = lax.dynamic_slice_in_dim(dt[:, :128], xl * 64, 64, 1)
    d = merge_data(got[:, :256].reshape(4, 4, 64, 640), wx, dx).astype(BF)

    d = d.reshape(4, 8, 8, 8, 2, 40).transpose(3, 4, 2, 0, 1, 5).reshape(128, 1280)
    st = pack(m2[:128], s2[:128], t2[:128]).reshape(1, 1024)
    op = jnp.concatenate([d, jnp.broadcast_to(st, (128, 1024))], 1)
    got = lax.all_to_all(op, YZ, 0, 0, tiled=True).reshape(8, 2, 8, 2304)
    got = got.transpose(0, 2, 1, 3).reshape(64, 2, 2304)
    ms, ss, ts = unpack(got[:, :, 1280:].reshape(64, 2, 8, 128).transpose(2, 0, 1, 3))
    M, S, T, w, dt = merge(ms, ss, ts)
    y = lax.axis_index("y")

    def mine(v):
        v = v.reshape(64, 2, 2, 8, 8)
        v = lax.dynamic_index_in_dim(v, xl, 2, keepdims=False)
        return lax.dynamic_index_in_dim(v, y, 3, keepdims=False).reshape(64, 16)

    d = got[:, :, :1280].reshape(64, 2, 4, 8, 40).transpose(0, 2, 1, 3, 4).reshape(64, 4, 16, 40)
    d = merge_data(d, mine(w), mine(dt))
    Sm = mine(jnp.broadcast_to(S[None], (64, 2, 128)))[0]
    embed_grad = d[1] + d[2] / Sm[:, None]
    out_grad = d[0]

    core = lax.axis_index("core")

    def rel(v):
        return jnp.concatenate([
            lax.dynamic_index_in_dim(v, core, 0, keepdims=False),
            lax.dynamic_index_in_dim(v, 1 - core, 0, keepdims=False)])

    M, S, T = rel(M), rel(S), rel(T)
    alpha = jnp.exp(m - M) / S
    disp = e * alpha[:, None]
    lg = (part + disp * (dc + (t - T)[:, None])).astype(BF)
    token_grad = (tn(lg, embed_all) + tn(disp.astype(BF), inputs_all)).astype(BF)
    return token_grad, embed_grad, out_grad


def solution(mesh):
    fine = Mesh(mesh.devices.reshape(2, 8, 2, 8, 2), ("xh", "z", "core", "y", "xl"))
    rows = P(("xh", "z", "core", "y", "xl"), None)
    slot = P(("y", "xl"), ("xh", "z", "core"))
    return jax.shard_map(
        per_device,
        mesh=fine,
        in_specs=(rows, slot, slot, rows, slot),
        out_specs=(rows, slot, slot),
        check_vma=False,
    )
```

time: 872 us -> 199 us (0.23)
  blocking collectives: 514 us -> 50.6 us
  waiting for transfers between devices: 323 us -> 44.5 us
  local copies, waits for them, and re-layouts: 4.16 us -> 40.4 us
  other arithmetic: 3.42 us -> 32.4 us
  starting transfers between devices: 0.08 us -> 18.6 us
  between operations: 14.7 us -> 1.38 us
    unnamed x3 -> x0, waiting for transfers between devices: 260 us -> none
    all_gather x6 -> x0, blocking collectives: 218 us -> none  [the longest x1 49.9 us: per_device(): lax.all_gather(slot_input_grad, 'seq', axis=1, tiled=True)]
    psum x2 -> x0, blocking collectives: 193 us -> none  [the longest x1 99.6 us: per_device(): lax.psum(jnp.sum(dispatch * dispatch_grad, axis=0), ('seq', 'exp'))]
    pmax x1 -> x0, blocking collectives: 103 us -> none  [per_device(): col_max = lax.pmax(local_max, ('seq', 'exp'))]
    reduce_scatter x1 -> x0, waiting for transfers between devices: 62.4 us -> none  [per_device(): lax.psum_scatter(jnp.stack([outputs_part, embed_part], axis=1), 'exp', sc...]
    all_to_all x0 -> x2, blocking collectives: none -> 50.6 us  [the longest x1 33 us: per_device(): got = lax.all_to_all(op, YZ, 0, 0, tiled=True)]
    all_to_all x0 -> x2, waiting for transfers between devices: none -> 39.5 us  [the longest x1 20.9 us: per_device(): got = lax.all_to_all(op, YZ, 0, 0, tiled=True).reshape(8, 2, 8, 2304)]
    all_to_all x0 -> x2, starting transfers between devices: none -> 10.7 us  [the longest x1 6.18 us: per_device(): got = lax.all_to_all(op, YZ, 0, 0, tiled=True).reshape(8, 2, 8, 2304)]
  transfers between devices with their start and end apart: 2 -> 5, of which waited for: 2 -> 4; matrix products, arithmetic and copies ran while one was open for 1% -> 2% of each run, Pallas kernels for 0% -> 0%
where the time goes in v1:
time: 199 us; the launch traced here: 198 us
  blocking collectives  50.6 us (25%)
  waiting for transfers between devices  44.5 us (22%)
  local copies, waits for them, and re-layouts  40.4 us (20%)
  other arithmetic  32.4 us (16%)
  starting transfers between devices  18.6 us (9%)
  matrix products  9.81 us (5%)
    all_to_all x1, blocking collectives, per_device(): got = lax.all_to_all(op, YZ, 0, 0, tiled=True)  33 us
    all_to_all x1, waiting for transfers between devices, per_device(): got = lax.all_to_all(op, YZ, 0, 0, tiled=True).reshape(8, 2, 8, 2304)  20.9 us
    all_to_all x1, waiting for transfers between devices, per_device(): got = lax.all_to_all(op, X, 0, 0, tiled=True)  18.6 us
    all_to_all x1, blocking collectives, per_device(): lax.all_to_all(jnp.broadcast_to(got[None], (4, 192, 640)), X, 0, 0, tiled...  17.6 us
    unnamed x45, local copies, waits for them, and re-layouts  9.88 us
    ppermute x3, starting transfers between devices, swap(): return lax.ppermute(x, 'core', [(0, 1), (1, 0)])  7.9 us
    all_to_all x1, starting transfers between devices, per_device(): got = lax.all_to_all(op, YZ, 0, 0, tiled=True).reshape(8, 2, 8, 2304)  6.18 us
    another operation x8, local copies, waits for them, and re-layouts, merge_data(): return jnp.stack([o, a, b, c], 0)  6.07 us
  transfers between devices with their start and end apart: 5, of which 4 were waited for; matrix products, arithmetic and copies ran while one was open for 2% of the time, Pallas kernels for 0%

profile of v1, /device:TPU:1, one launch (start us, length us, event | category | flops | bytes accessed | tf_op | source)
XLA Modules:
  0.0 197.7 jit_solution(489740824847120449)
XLA Ops:
  3.1 33.0 %all_to_all.28 = bf16[128,2,480]{2,1,0:T(2,128)(2,1)S(1)} all-to-all(bf16[128,2,480]{2,1,0:T(2,128)(2,1)S(1)} %reshape.453), channel_id=1, replica_groups=mesh['xh'=2,'z'=8,'core'=2,'y'=8,'xl'=2] {'z','core','y'}, dimensions={0} | all-to-all | bytes 491520 | tf_op jit(solution)/shard_map/all_to_all | solution.py:71
  36.5 1.6 reduce.9
  40.6 17.6 %all_to_all.29 = bf16[4,192,640]{2,1,0:T(8,128)(2,1)S(1)} all-to-all(bf16[4,192,640]{2,1,0:T(8,128)(2,1)S(1)} %broadcast_in_dim.17), channel_id=1, replica_groups=mesh['xh'=2,'z'=8,'core'=2,'y'=8,'xl'=2] {'xh','xl'}, dimensions={0} | all-to-all | bytes 1966080 | tf_op jit(solution)/shard_map/all_to_all | solution.py:73
  58.2 3.6 %collective-permute-start = (bf16[4,192,640]{2,1,0:T(8,128)(2,1)S(1)}, bf16[4,192,640]{2,1,0:T(8,128)(2,1)S(1)}, u32[]{:S(2)}, u32[]{:S(2)}) collective-permute-start(bf16[4,192,640]{2,1,0:T(8,128)(2,1)S(1)} %all_to_all.29), channel_id=1, source_target_pairs={{0,16},{16,0},{1,17},{17,1},{2,18},{18,2},{3,19},{19,3},{4,20},{20... | collective-permute-start | bytes 2949128 | tf_op jit(solution)/shard_map/ppermute | solution.py:64
  61.8 2.0 %collective-permute-done = bf16[4,192,640]{2,1,0:T(8,128)(2,1)S(1)} collective-permute-done((bf16[4,192,640]{2,1,0:T(8,128)(2,1)S(1)}, bf16[4,192,640]{2,1,0:T(8,128)(2,1)S(1)}, u32[]{:S(2)}, u32[]{:S(2)}) %collective-permute-start) | collective-permute-done | bytes 983072 | tf_op jit(solution)/shard_map/ppermute | solution.py:64
  68.6 1.4 fusion.1
  70.6 1.4 fusion.66
  72.0 2.3 %collective-permute-start.2 = (bf16[8,256]{1,0:T(8,128)(2,1)S(1)}, bf16[8,256]{1,0:T(8,128)(2,1)S(1)}, u32[]{:S(2)}, u32[]{:S(2)}) collective-permute-start(bf16[8,256]{1,0:T(8,128)(2,1)S(1)} %stack.155), channel_id=1, source_target_pairs={{0,16},{16,0},{1,17},{17,1},{2,18},{18,2},{3,19},{19,3},{4,20},{20... | collective-permute-start | bytes 12296 | tf_op jit(solution)/shard_map/ppermute | solution.py:64
  74.3 1.6 fusion.2
  77.4 1.7 slice_bitcast_fusion.2
  79.1 2.0 %collective-permute-start.1 = (bf16[4,128,1280]{2,1,0:T(8,128)(2,1)}, bf16[4,128,1280]{2,1,0:T(8,128)(2,1)}, u32[]{:S(2)}, u32[]{:S(2)}) collective-permute-start(bf16[4,128,1280]{2,1,0:T(8,128)(2,1)} %get-tuple-element.38), channel_id=1, source_target_pairs={{0,16},{16,0},{1,17},{17,1},{2,18},{18,2},{3,19},{19,3},{4,20},{20... | collective-permute-start | bytes 3932168 | tf_op jit(solution)/shard_map/ppermute | solution.py:64
  81.4 3.0 %collective-permute-done.1 = bf16[4,128,1280]{2,1,0:T(8,128)(2,1)} collective-permute-done((bf16[4,128,1280]{2,1,0:T(8,128)(2,1)}, bf16[4,128,1280]{2,1,0:T(8,128)(2,1)}, u32[]{:S(2)}, u32[]{:S(2)}) %collective-permute-start.1) | collective-permute-done | bytes 1310752 | tf_op jit(solution)/shard_map/ppermute | solution.py:64
  84.4 2.1 %maximum_convert_fusion = f32[2,4,128,1280]{3,2,1,0:T(8,128)S(1)} fusion(bf16[1,4,128,1280]{3,2,1,0:T(8,128)(2,1)} %bitcast.17, bf16[1,4,128,1280]{3,2,1,0:T(8,128)(2,1)} %get-tuple-element.37), kind=kLoop, calls=%fused_computation.3 | loop fusion | flops 2621440 | bytes 7864320 | tf_op jit(solution)/shard_map/convert_element_type | solution.py:53
  88.9 1.8 stack.160
  91.5 3.8 %maximum_bitcast_fusion.1 = bf16[2,2,4,64,640]{4,0,3,1,2:T(2,128)(2,1)S(1)} fusion(bf16[1,2,64,2,640]{4,3,2,1,0:T(2,128)(2,1)} %stack.160, bf16[1,2,64,2,640]{4,3,2,1,0:T(2,128)(2,1)S(1)} %stack.159, bf16[1,2,64,2,640]{4,3,2,1,0:T(2,128)(2,1)S(1)} %stack.154, bf16[1,2,64,2,640]{4,3,2,1,0:T(2,128)(2,1)} %stack.153), kind=kLoop, calls=%fused_computation.22 | loop fusion | flops 1966080 | bytes 2621440 | tf_op jit(solution)/shard_map/transpose | solution.py:105
  96.8 4.5 %all-to-all-start.2 = ((bf16[4,272,640]{2,1,0:T(8,128)(2,1)}), bf16[4,272,640]{2,1,0:T(8,128)(2,1)}, u32[]{:S(2)}, u32[]{:S(2)}) async-start(bf16[4,272,640]{2,1,0:T(8,128)(2,1)} %pad_maximum_fusion.1), calls=%async_computation.2 | async-start | bytes 2785280 | tf_op jit(solution)/shard_map/all_to_all | solution.py:108
  101.3 18.6 %all-to-all-done.2 = bf16[4,272,640]{2,1,0:T(8,128)(2,1)} async-done(((bf16[4,272,640]{2,1,0:T(8,128)(2,1)}), bf16[4,272,640]{2,1,0:T(8,128)(2,1)}, u32[]{:S(2)}, u32[]{:S(2)}) %all-to-all-start.2) | async-done | bytes 1392672 | tf_op jit(solution)/shard_map/all_to_all | solution.py:108
  122.7 1.6 bitcast_convert_fusion
  127.6 2.2 %maximum_bitcast_fusion.2 = bf16[8,2,8,4,8,40]{5,1,0,2,4,3:T(2,128)(2,1)S(1)} fusion(bf16[1,8,8,8,2,40]{5,4,3,2,1,0:T(2,128)(2,1)S(1)} %stack.166, bf16[1,8,8,8,2,40]{5,4,3,2,1,0:T(2,128)(2,1)S(1)} %stack.165, bf16[1,8,8,8,2,40]{5,4,3,2,1,0:T(2,128)(2,1)S(1)} %stack.164, bf16[1,8,8,8,2,40]{5,4,3,2,1,0:T(2,128)(2,1)S(1)} %stack.163), kind=kLoop, calls=%fused_computation.24 | loop fusion | flops 491520 | bytes 655360 | tf_op jit(solution)/shard_map/transpose | solution.py:116
  130.5 2.6 %reshape.443 = bf16[128,1280]{1,0:T(8,128)(2,1)} reshape(bf16[8,2,8,4,8,40]{5,4,3,2,1,0:T(8,128)(2,1)S(1)} %copy.123) | data formatting | bytes 655360 | tf_op jit(solution)/shard_map/reshape | solution.py:116
  134.8 1.7 reduce.13
  136.6 2.6 %reshape.455 = bf16[128,2,1152]{2,1,0:T(2,128)(2,1)} reshape(bf16[128,2304]{1,0:T(8,128)(2,1)} %reduce.13) | data formatting | bytes 1179648
  139.1 6.2 %all-to-all-start.3 = ((bf16[128,2,1152]{2,1,0:T(2,128)(2,1)}), bf16[128,2,1152]{2,1,0:T(2,128)(2,1)S(1)}, u32[]{:S(2)}, u32[]{:S(2)}) async-start(bf16[128,2,1152]{2,1,0:T(2,128)(2,1)} %reshape.455), calls=%async_computation.3 | async-start | bytes 1179648 | tf_op jit(solution)/shard_map/all_to_all | solution.py:119
  145.3 20.9 %all-to-all-done.3 = bf16[128,2,1152]{2,1,0:T(2,128)(2,1)S(1)} async-done(((bf16[128,2,1152]{2,1,0:T(2,128)(2,1)}), bf16[128,2,1152]{2,1,0:T(2,128)(2,1)S(1)}, u32[]{:S(2)}, u32[]{:S(2)}) %all-to-all-start.3) | async-done | bytes 589856 | tf_op jit(solution)/shard_map/all_to_all | solution.py:119
  166.2 1.8 reshape.456
  171.2 1.4 copy.126
  173.9 2.2 %fusion.70 = (f32[2,128]{1,0:T(2,128)S(1)}, f32[2,128]{1,0:T(2,128)}, f32[1,64,2,128]{1,3,2,0:T(8,128)}) fusion(f32[8,64,2,128]{1,3,2,0:T(8,128)S(1)} %bitcast.219, f32[2,128]{1,0:T(2,128)S(1)} %get-tuple-element.25, f32[1,64,2,128]{1,3,2,0:T(8,128)} %get-tuple-element.26), kind=kLoop, calls=%fused_computation.181 | loop fusion | flops 130560 | bytes 461824 | tf_op jit(solution)/shard_map/reduce_sum | solution.py:47
  179.5 1.4 constant_dynamic-slice_fusion.1
  182.2 2.5 %copy.127 = f32[64,2,1280]{0,2,1:T(8,128)} copy(f32[64,2,1280]{2,0,1:T(8,128)} %slice_convert_fusion) | data formatting | bytes 1310720 | tf_op jit(solution)/shard_map/convert_element_type | solution.py:53
  184.8 1.5 copy.128
  191.6 1.5 fusion.17
  193.2 1.7 fusion
  (135 shorter events, 42.7 us)
Async XLA Ops:
  0.6 65.9 %copy-start = (bf16[512,1280]{1,0:T(8,128)(2,1)S(1)}, bf16[512,1280]{1,0:T(8,128)(2,1)}, u32[]{:S(2)}) copy-start(bf16[512,1280]{1,0:T(8,128)(2,1)} %param.5) | copy-start | bytes 3932164
  58.2 5.6 %collective-permute-start = (bf16[4,192,640]{2,1,0:T(8,128)(2,1)S(1)}, bf16[4,192,640]{2,1,0:T(8,128)(2,1)S(1)}, u32[]{:S(2)}, u32[]{:S(2)}) collective-permute-start(bf16[4,192,640]{2,1,0:T(8,128)(2,1)S(1)} %all_to_all.29), channel_id=1, source_target_pairs={{0,16},{16,0},{1,17},{17,1},{2,18},{18,2},{3,19},{19,3},{4,20},{20... | collective-permute-start | bytes 2949128 | tf_op jit(solution)/shard_map/ppermute | solution.py:64
  66.5 4.0 %copy-start.3 = (bf16[32,8,2,640]{3,1,2,0:T(8,128)(2,1)}, bf16[32,8,2,640]{3,1,2,0:T(8,128)(2,1)S(1)}, u32[]{:S(2)}) copy-start(bf16[32,8,2,640]{3,1,2,0:T(8,128)(2,1)S(1)} %copy.148) | copy-start | bytes 1966084
  66.5 1.6 copy-start.9
  67.3 7.0 %copy-start.14 = (f32[512]{0:T(512)}, f32[512]{0:T(512)S(1)}, u32[]{:S(2)}) copy-start(f32[512]{0:T(512)S(1)} %get-tuple-element.16) | copy-start | bytes 6148
  68.6 1.9 copy-start.5
  71.9 4.0 %copy-start.15 = (f32[512]{0:T(512)}, f32[512]{0:T(512)S(1)}, u32[]{:S(2)}) copy-start(f32[512]{0:T(512)S(1)} %get-tuple-element.15) | copy-start | bytes 6148
  71.9 4.1 %copy-start.13 = (f32[256]{0:T(256)}, f32[256]{0:T(256)S(1)}, u32[]{:S(2)}) copy-start(f32[256]{0:T(256)S(1)} %div.93) | copy-start | bytes 3076
  72.0 9.1 %collective-permute-start.2 = (bf16[8,256]{1,0:T(8,128)(2,1)S(1)}, bf16[8,256]{1,0:T(8,128)(2,1)S(1)}, u32[]{:S(2)}, u32[]{:S(2)}) collective-permute-start(bf16[8,256]{1,0:T(8,128)(2,1)S(1)} %stack.155), channel_id=1, source_target_pairs={{0,16},{16,0},{1,17},{17,1},{2,18},{18,2},{3,19},{19,3},{4,20},{20... | collective-permute-start | bytes 12296 | tf_op jit(solution)/shard_map/ppermute | solution.py:64
  74.3 1.7 copy-start.7
  76.0 1.1 copy-start.10
  79.1 5.3 %collective-permute-start.1 = (bf16[4,128,1280]{2,1,0:T(8,128)(2,1)}, bf16[4,128,1280]{2,1,0:T(8,128)(2,1)}, u32[]{:S(2)}, u32[]{:S(2)}) collective-permute-start(bf16[4,128,1280]{2,1,0:T(8,128)(2,1)} %get-tuple-element.38), channel_id=1, source_target_pairs={{0,16},{16,0},{1,17},{17,1},{2,18},{18,2},{3,19},{19,3},{4,20},{20... | collective-permute-start | bytes 3932168 | tf_op jit(solution)/shard_map/ppermute | solution.py:64
  96.8 23.1 %all-to-all-start.2 = ((bf16[4,272,640]{2,1,0:T(8,128)(2,1)}), bf16[4,272,640]{2,1,0:T(8,128)(2,1)}, u32[]{:S(2)}, u32[]{:S(2)}) async-start(bf16[4,272,640]{2,1,0:T(8,128)(2,1)} %pad_maximum_fusion.1), calls=%async_computation.2 | async-start | bytes 2785280 | tf_op jit(solution)/shard_map/all_to_all | solution.py:108
  129.8 3.3 %copy-start.16 = (bf16[1,128]{1,0:T(2,128)(2,1)S(1)}, bf16[1,128]{1,0:T(2,128)(2,1)}, u32[]{:S(2)}) copy-start(bf16[1,128]{1,0:T(2,128)(2,1)} %get-tuple-element.64) | copy-start | bytes 772
  139.1 27.1 %all-to-all-start.3 = ((bf16[128,2,1152]{2,1,0:T(2,128)(2,1)}), bf16[128,2,1152]{2,1,0:T(2,128)(2,1)S(1)}, u32[]{:S(2)}, u32[]{:S(2)}) async-start(bf16[128,2,1152]{2,1,0:T(2,128)(2,1)} %reshape.455), calls=%async_computation.3 | async-start | bytes 1179648 | tf_op jit(solution)/shard_map/all_to_all | solution.py:119
  184.8 6.8 %copy-start.6 = (f32[256,512]{1,0:T(8,128)S(1)}, f32[256,512]{1,0:T(8,128)}, u32[]{:S(2)}) copy-start(f32[256,512]{1,0:T(8,128)} %copy-done.5) | copy-start | bytes 1572868
  184.8 6.8 %copy-start.8 = (f32[256,512]{1,0:T(8,128)S(1)}, f32[256,512]{1,0:T(8,128)}, u32[]{:S(2)}) copy-start(f32[256,512]{1,0:T(8,128)} %get-tuple-element.89) | copy-start | bytes 1572868
  186.3 1.1 copy-start.1
  191.6 1.5 copy-start.4
  193.1 1.8 copy-start.11
  193.1 2.7 %copy-start.12 = (f32[2,1,8,1]{3,2,1,0:T(8,128)S(1)}, f32[2,1,8,1]{3,2,1,0:T(8,128)}, u32[]{:S(2)}) copy-start(f32[2,1,8,1]{3,2,1,0:T(8,128)} %constant_dynamic-slice_fusion) | copy-start | bytes 196
  193.1 3.7 %copy-start.2 = (f32[64,4,2,8,40]{0,4,3,2,1:T(8,128)S(1)}, f32[64,4,2,8,40]{0,4,3,2,1:T(8,128)}, u32[]{:S(2)}) copy-start(f32[64,4,2,8,40]{0,4,3,2,1:T(8,128)} %copy-done.1) | copy-start | bytes 1966084
  193.1 3.8 %copy-start.17 = (f32[16]{0:T(128)S(1)}, f32[16]{0:T(128)}, u32[]{:S(2)}) copy-start(f32[16]{0:T(128)} %div.101) | copy-start | bytes 196

commit v2 on v0

v2 whole, which is shorter than its diff:
```python
import jax
import jax.numpy as jnp
from jax import lax
from jax.experimental import pallas as pl
from jax.experimental.pallas import tpu as pltpu
from jax.sharding import Mesh, PartitionSpec as P

BF = jnp.bfloat16
F32 = jnp.float32
YZ = ("z", "core", "y")
X = ("xh", "xl")
LANES = 128
WIDE = 40
VMEM_BYTES = 32 * 1024 * 1024


def nt(a, b):
    return lax.dot_general(a, b, (((1,), (1,)), ((), ())), preferred_element_type=F32)


def nn(a, b):
    return lax.dot_general(a, b, (((1,), (0,)), ((), ())), preferred_element_type=F32)


def tn(a, b):
    return lax.dot_general(a, b, (((0,), (0,)), ((), ())), preferred_element_type=F32)


def roll(x, shift):
    shift %= LANES
    return x if shift == 0 else pltpu.roll(x, shift, axis=x.ndim - 1)


def lane_of(shape):
    return lax.broadcasted_iota(jnp.int32, shape, len(shape) - 1)


def columns(p, n, first):
    shape = (n, 8, LANES)
    pick = lane_of(shape) == lax.broadcasted_iota(jnp.int32, shape, 0) + first
    x = jnp.where(pick, jnp.broadcast_to(p[None], shape), 0.0)
    return jnp.sum(x, axis=2, keepdims=True).reshape(n * 8, 1)


def packed(v, n, first):
    shape = (n, 8, LANES)
    pick = lane_of(shape) == lax.broadcasted_iota(jnp.int32, shape, 0) + first
    x = jnp.where(pick, jnp.broadcast_to(v.reshape(n, 8, 1), shape), 0.0)
    return jnp.sum(x, axis=0)


def split(x, n):
    parts = []
    for _ in range(n):
        part = x.astype(BF)
        parts.append(part)
        x = x - part.astype(F32)
    return parts


def stat_rows(p):
    a, b, c = split(p, 3)
    rest = jnp.zeros((8, 640 - 3 * LANES), BF)
    top = jnp.concatenate([a, b, c, rest], axis=1).astype(F32)
    return jnp.concatenate([top, jnp.zeros((8, 640), F32)], axis=0).astype(BF)


def stat_read(rows):
    f = rows.astype(F32)[:8]
    return f[:, :LANES] + f[:, LANES:2 * LANES] + f[:, 2 * LANES:3 * LANES]


def pieces_kernel(e_ref, o_ref, i_ref, out_ref):
    def at(ref, k):
        x = ref[...].astype(F32)
        x = jnp.concatenate([x, jnp.zeros((16, LANES - WIDE), F32)], axis=1)
        return roll(x, k * WIDE)

    x = at(e_ref, 0) + at(o_ref, 1) + at(i_ref, 2)
    for half in range(2):
        rows = x[half * 8:half * 8 + 8]
        many = jnp.broadcast_to(rows[None], (8, 8, LANES)).astype(BF)
        for z in range(8):
            at_row = (z * 2 + half) * 8
            out_ref[at_row:at_row + 8] = many


def widen_kernel(got_ref, out_ref):
    lane = lane_of((64, LANES))
    blocks = [got_ref[k * 8:(k + 1) * 8].astype(F32).reshape(64, LANES) for k in range(16)]
    for a in range(3):
        tiles = [None] * 5
        for k in range(16):
            x = roll(blocks[k], WIDE * (k - a))
            first, last = WIDE * k, WIDE * k + WIDE
            for j in range(first // LANES, (last - 1) // LANES + 1):
                lo = max(first - j * LANES, 0)
                tiles[j] = x if tiles[j] is None else jnp.where(lane >= lo, x, tiles[j])
        whole = jnp.concatenate(tiles, axis=1).astype(BF)
        for j in range(4):
            out_ref[j, a * 64:(a + 1) * 64, :] = whole


def main_kernel(own_ref, sib_ref, tok_ref, og_ref,
                g_ref, e_ref, part_ref, dc_ref, m_ref, t_ref, p_ref, down_ref, dsib_ref, outs_ref):
    for h, ref in ((0, own_ref), (1, sib_ref)):
        for xl in range(2):
            for xh in range(2):
                rows = pl.ds(h * 128 + xl * 64, 64)
                cols = pl.ds(xh * 640, 640)
                j = xh * 2 + xl
                g_ref[rows, cols] = ref[j, 0:64, :]
                outs_ref[rows, cols] = ref[j, 64:128, :]
                g_ref[pl.ds(256 + h * 128 + xl * 64, 64), cols] = ref[j, 128:192, :]
    tok = tok_ref[...]
    og = og_ref[...]
    cgrad = nt(outs_ref[...], og)
    logits = nt(g_ref[0:256, :], tok)
    dgrad = nt(g_ref[256:512, :], tok)
    raised = jnp.exp(logits - jnp.max(logits, axis=0, keepdims=True))
    combine = raised / jnp.sum(raised, axis=0, keepdims=True)
    row = jnp.sum(combine * cgrad, axis=0, keepdims=True)
    part = combine * (cgrad - row)
    m = jnp.max(logits, axis=1, keepdims=True)
    e = jnp.exp(logits - m)
    s = jnp.sum(e, axis=1, keepdims=True)
    t = jnp.sum(e * dgrad, axis=1, keepdims=True) / s
    dc = dgrad - t
    e_ref[...] = e
    part_ref[...] = part
    dc_ref[...] = dc
    m_ref[...] = m
    t_ref[...] = t
    p = packed(m, 32, 0) + packed(s, 32, 32) + packed(t, 32, 64)
    p_ref[...] = p
    for k, (left, right) in enumerate(((combine, og), (part, tok), (e * dc, tok), (e, tok))):
        x = nn(left.astype(BF), right).astype(BF)
        down_ref[k * 128:(k + 1) * 128, :] = x[:128]
        dsib_ref[k * 128:(k + 1) * 128, :] = x[128:]
    dsib_ref[512:528, 0:640] = stat_rows(p)
    dsib_ref[512:528, 640:1280] = jnp.zeros((16, 640), BF)


def merge_stats(ps, groups, exact=True):
    ms = ps
    ss = [roll(p, -groups) for p in ps]
    ts = [roll(p, -2 * groups) for p in ps]
    lane = lane_of((8, LANES))
    ok = lane < groups
    ms = [jnp.where(ok, v, 0.0) for v in ms]
    ss = [jnp.where(ok, v, 1.0) for v in ss]
    ts = [jnp.where(ok, v, 0.0) for v in ts]
    top = ms[0]
    for v in ms[1:]:
        top = jnp.maximum(top, v)
    if not exact:
        top = sum(v.astype(F32) for v in split(top, 2))
    ws = [jnp.exp(v - top) for v in ms]
    total = sum(w * s for w, s in zip(ws, ss))
    mean = sum(w * s * t for w, s, t in zip(ws, ss, ts)) / total
    if not exact:
        mean = sum(v.astype(F32) for v in split(mean, 2))
    return top, total, mean, ws, [t - mean for t in ts]


def core_kernel(own_ref, got_ref, p_ref, out_ref):
    lane = lane_of((8, LANES))
    q = stat_read(got_ref[512:528, 0:640])
    q = jnp.where(lane % 32 < 16, roll(q, -16), roll(q, 16))
    top, total, mean, ws, ds = merge_stats([p_ref[...], q], 32)
    ok = lane < 32
    p = jnp.where(ok, top, 0.0) + roll(jnp.where(ok, total, 0.0), 32) + roll(jnp.where(ok, mean, 0.0), 64)
    stats = stat_rows(p)
    w1, w2 = columns(ws[0], 16, 0), columns(ws[1], 16, 0)
    d1, d2 = columns(ds[0], 16, 0), columns(ds[1], 16, 0)

    def rows(ref, k):
        return ref[k * 128:(k + 1) * 128, :].astype(F32)

    def put(k, x):
        x = x.astype(BF)
        for xh in range(2):
            for xl in range(2):
                out_ref[xh * 2 + xl, k * 64:(k + 1) * 64, :] = x[xl * 64:(xl + 1) * 64, xh * 640:(xh + 1) * 640]

    put(0, rows(own_ref, 0) + rows(got_ref, 0))
    put(1, rows(own_ref, 1) + rows(got_ref, 1))
    c1, c2 = w1 * rows(own_ref, 3), w2 * rows(got_ref, 3)
    put(2, w1 * rows(own_ref, 2) + w2 * rows(got_ref, 2) + d1 * c1 + d2 * c2)
    put(3, c1 + c2)
    for j in range(4):
        out_ref[j, 256:272, :] = stats


def x_kernel(got_ref, out_ref):
    xl = lax.axis_index("xl")
    top, total, mean, ws, ds = merge_stats([stat_read(got_ref[j, 256:272, :]) for j in range(4)], 32, False)
    ws = [columns(w, 8, xl * 8) for w in ws]
    ds = [columns(d, 8, xl * 8) for d in ds]

    def rows(j, k):
        return got_ref[j, k * 64:(k + 1) * 64, :].astype(F32)

    o = sum(rows(j, 0) for j in range(4))
    a = sum(rows(j, 1) for j in range(4))
    cs = [ws[j] * rows(j, 3) for j in range(4)]
    b = sum(ws[j] * rows(j, 2) + ds[j] * cs[j] for j in range(4))
    c = sum(cs)
    lane8 = lane_of((8, LANES))
    ok = lane8 < 16
    p = jnp.where(ok, top, 0.0) + roll(jnp.where(ok, total, 0.0), 16) + roll(jnp.where(ok, mean, 0.0), 32)
    hi, mid = split(p, 2)
    stats = roll(hi.astype(F32), 32) + roll(mid.astype(F32), 80)
    stats = jnp.broadcast_to(stats[None], (8, 8, LANES)).reshape(64, LANES)
    lane = lane_of((64, LANES))
    for k in range(16):
        first = WIDE * k
        j = first // LANES
        cut = (j + 1) * LANES - first
        chunks = []
        for n, x in enumerate((o, a, b, c)):
            v = x[:, j * LANES:(j + 1) * LANES]
            if cut < WIDE:
                v = jnp.where(lane < WIDE - cut, x[:, (j + 1) * LANES:(j + 2) * LANES], v)
            chunks.append(roll(v, WIDE * n - first))
        low = jnp.where(lane < 40, chunks[0], jnp.where(lane < 80, chunks[1], jnp.where(lane < 120, chunks[2], chunks[3])))
        high = jnp.where(lane < 32, chunks[3], stats)
        out_ref[k * 8:(k + 1) * 8, :, 0:LANES] = low.reshape(8, 8, LANES).astype(BF)
        out_ref[k * 8:(k + 1) * 8, :, LANES:2 * LANES] = high.reshape(8, 8, LANES).astype(BF)


def last_kernel(got_ref, g_ref, e_ref, part_ref, dc_ref, m_ref, t_ref, tg_ref, eg_ref, og_ref, l_ref):
    xl, y, core = lax.axis_index("xl"), lax.axis_index("y"), lax.axis_index("core")
    big = (8, 2, 8, 8, LANES)
    t0 = got_ref[:, :, 0:LANES].astype(F32).reshape(big)
    t1 = got_ref[:, :, LANES:2 * LANES].astype(F32).reshape(1024, LANES)
    p = t1 + roll(t1, -48)
    s = roll(p, -16).reshape(big)
    t = roll(p, -32).reshape(big)
    m = p.reshape(big)
    t1 = t1.reshape(big)
    lane = lane_of((8, LANES))
    ok = (lane >= 32) & (lane < 48)
    m = jnp.where(ok, m, 0.0)
    s = jnp.where(ok, s, 1.0)
    t = jnp.where(ok, t, 0.0)
    top = jnp.max(m, axis=(0, 2))
    w = jnp.exp(m - top[None, :, None])
    ws = w * s
    total = jnp.sum(ws, axis=(0, 2))
    mean = jnp.sum(ws * t, axis=(0, 2)) / total
    dt = t - mean[None, :, None]
    mine = lane == 32 + xl * 8 + y

    def pick(v):
        return jnp.sum(jnp.where(mine, v, 0.0), axis=-1, keepdims=True)

    wm = pick(w)
    wd = wm * pick(dt)
    acc0 = jnp.sum(t0 * jnp.where(lane < 80, 1.0, jnp.where(lane < 120, wm, wd)), axis=(0, 2))
    acc1 = jnp.sum(jnp.where(lane < 32, t1 * wd, 0.0), axis=(0, 2))
    for c in range(2):
        q = acc0[c]
        last = jnp.where(lane < 8, roll(q, -120), roll(acc1[c], 8))
        grad = roll(q, -40) + (roll(q, -80) + last) / pick(total[c])
        eg_ref[c * 8:(c + 1) * 8, :] = grad[:, 0:WIDE]
        og_ref[c * 8:(c + 1) * 8, :] = q[:, 0:WIDE]

    for h in range(2):
        second = (core + h) == 1

        def cols(v):
            return columns(jnp.where(second, v[1], v[0]), 16, 32)

        at = pl.ds(h * 128, 128)
        alpha = jnp.exp(m_ref[at, :] - cols(top)) / cols(total)
        shift = t_ref[at, :] - cols(mean)
        disp = e_ref[at, :] * alpha
        l_ref[at, :] = (part_ref[at, :] + disp * (dc_ref[at, :] + shift)).astype(BF)
        l_ref[pl.ds(256 + h * 128, 128), :] = disp.astype(BF)
    tg_ref[...] = tn(l_ref[...], g_ref[...]).astype(BF)


def call(kernel, outs, *args, scratch=(), flops=0):
    vm = pl.BlockSpec(memory_space=pltpu.VMEM)
    many = isinstance(outs, list)
    return pl.pallas_call(
        kernel,
        out_shape=outs,
        in_specs=[vm] * len(args),
        out_specs=[vm] * len(outs) if many else vm,
        scratch_shapes=list(scratch),
        compiler_params=pltpu.CompilerParams(vmem_limit_bytes=VMEM_BYTES),
    )(*args)


def shape(*dims, dtype=BF):
    return jax.ShapeDtypeStruct(dims, dtype)


def swap(x):
    return lax.ppermute(x, "core", [(0, 1), (1, 0)])


def per_device(tokens, slot_embed, slot_outputs, output_grad, slot_input_grad):
    op = call(pieces_kernel, shape(128, 8, LANES), slot_embed, slot_outputs, slot_input_grad)
    got = lax.all_to_all(op, YZ, 0, 0, tiled=True)
    op = call(widen_kernel, shape(4, 192, 640), got)
    own = lax.all_to_all(op, X, 0, 0, tiled=True)
    sib = swap(own)
    g, e, part, dc, m, t, p, down, dsib = call(
        main_kernel,
        [shape(512, 1280), shape(256, 512, dtype=F32), shape(256, 512, dtype=F32), shape(256, 512, dtype=F32),
         shape(256, 1, dtype=F32), shape(256, 1, dtype=F32), shape(8, LANES, dtype=F32),
         shape(512, 1280), shape(528, 1280)],
        own, sib, tokens, output_grad,
        scratch=[pltpu.VMEM((256, 1280), BF)])
    op = call(core_kernel, shape(4, 272, 640), down, swap(dsib), p)
    got = lax.all_to_all(op, X, 0, 0, tiled=True)
    op = call(x_kernel, shape(128, 8, 2 * LANES), got)
    got = lax.all_to_all(op, YZ, 0, 0, tiled=True)
    return call(
        last_kernel,
        [shape(512, 1280), shape(16, WIDE, dtype=F32), shape(16, WIDE, dtype=F32)],
        got, g, e, part, dc, m, t,
        scratch=[pltpu.VMEM((512, 512), BF)])


def solution(mesh):
    fine = Mesh(mesh.devices.reshape(2, 8, 2, 8, 2), ("xh", "z", "core", "y", "xl"))
    rows = P(("xh", "z", "core", "y", "xl"), None)
    slot = P(("y", "xl"), ("xh", "z", "core"))
    return jax.shard_map(
        per_device,
        mesh=fine,
        in_specs=(rows, slot, slot, rows, slot),
        out_specs=(rows, slot, slot),
        check_vma=False,
    )
```

time: 872 us -> 118 us (0.14)
  blocking collectives: 514 us -> 97.3 us
  waiting for transfers between devices: 323 us -> 4.87 us
  between operations: 14.7 us -> 0.7 us
  matrix products: 12.4 us -> 0 us
    unnamed x3 -> x0, waiting for transfers between devices: 260 us -> none
    all_gather x6 -> x0, blocking collectives: 218 us -> none  [the longest x1 49.9 us: per_device(): lax.all_gather(slot_input_grad, 'seq', axis=1, tiled=True)]
    psum x2 -> x0, blocking collectives: 193 us -> none  [the longest x1 99.6 us: per_device(): lax.psum(jnp.sum(dispatch * dispatch_grad, axis=0), ('seq', 'exp'))]
    pmax x1 -> x0, blocking collectives: 103 us -> none  [per_device(): col_max = lax.pmax(local_max, ('seq', 'exp'))]
    all_to_all x0 -> x4, blocking collectives: none -> 97.3 us  [the longest x2 58.8 us: per_device(): got = lax.all_to_all(op, YZ, 0, 0, tiled=True)]
    reduce_scatter x1 -> x0, waiting for transfers between devices: 62.4 us -> none  [per_device(): lax.psum_scatter(jnp.stack([outputs_part, embed_part], axis=1), 'exp', sc...]
    dot_general x7 -> x0, matrix products: 12.4 us -> none  [the longest x2 3.74 us: contract_first(): lax.dot_general(left, right, (((0,), (0,)), ((), ())), preferred_element_...]
  transfers between devices with their start and end apart: 2 -> 2, of which waited for: 2 -> 2; matrix products, arithmetic and copies ran while one was open for 1% -> 0% of each run, Pallas kernels for 0% -> 0%
where the time goes in v2:
time: 118 us
  blocking collectives  97.3 us (82%)
  Pallas kernels  7.35 us (6%)
  starting transfers between devices  5.71 us (5%)
  waiting for transfers between devices  4.87 us (4%)
  local copies, waits for them, and re-layouts  2.06 us (2%)
    all_to_all x2, blocking collectives, per_device(): got = lax.all_to_all(op, YZ, 0, 0, tiled=True)  58.8 us
    all_to_all x1, blocking collectives, per_device(): got = lax.all_to_all(op, X, 0, 0, tiled=True)  20.7 us
    all_to_all x1, blocking collectives, per_device(): own = lax.all_to_all(op, X, 0, 0, tiled=True)  17.8 us
    pallas_call x6, Pallas kernels, call(): pl.pallas_call(kernel, out_shape=outs, in_specs=[vm] * len(args), out_spe...  7.35 us
    ppermute x2, starting transfers between devices, swap(): return lax.ppermute(x, 'core', [(0, 1), (1, 0)])  5.71 us
    ppermute x2, waiting for transfers between devices, swap(): return lax.ppermute(x, 'core', [(0, 1), (1, 0)])  4.87 us
  transfers between devices with their start and end apart: 2, of which 2 were waited for; matrix products, arithmetic and copies ran while one was open for 0% of the time, Pallas kernels for 0%

profile of v2, /device:TPU:1, one launch (start us, length us, event | category | flops | bytes accessed | tf_op | source)
XLA Modules:
  0.0 118.0 jit_solution(8252116885497821521)
XLA Ops:
  0.6 0.0 copy-start.2
  0.6 0.7 copy-done.2
  1.3 0.0 copy-start.3
  1.3 0.7 copy-done.3
  2.0 0.0 copy-start.4
  2.0 0.7 copy-done.4
  2.7 0.1 shard_map.76
  2.8 33.0 %all_to_all.20.got_ref = bf16[128,8,128]{2,1,0:T(8,128)(2,1)S(1)} all-to-all(bf16[128,8,128]{2,1,0:T(8,128)(2,1)S(1)} %shard_map.76), channel_id=1, replica_groups=mesh['xh'=2,'z'=8,'core'=2,'y'=8,'xl'=2] {'z','core','y'}, dimensions={0} | all-to-all | bytes 524288 | tf_op jit(solution)/shard_map/all_to_all | solution.py:307
  35.7 0.0 copy-start
  35.7 0.0 copy-start.1
  35.7 0.3 shard_map.77
  36.0 17.8 %all_to_all.21.own_ref = bf16[4,192,640]{2,1,0:T(8,128)(2,1)S(1)} all-to-all(bf16[4,192,640]{2,1,0:T(8,128)(2,1)S(1)} %shard_map.77), channel_id=1, replica_groups=mesh['xh'=2,'z'=8,'core'=2,'y'=8,'xl'=2] {'xh','xl'}, dimensions={0} | all-to-all | bytes 1966080 | tf_op jit(solution)/shard_map/all_to_all | solution.py:309
  53.8 3.4 %collective-permute-start = (bf16[4,192,640]{2,1,0:T(8,128)(2,1)S(1)}, bf16[4,192,640]{2,1,0:T(8,128)(2,1)S(1)}, u32[]{:S(2)}, u32[]{:S(2)}) collective-permute-start(bf16[4,192,640]{2,1,0:T(8,128)(2,1)S(1)} %all_to_all.21.own_ref), channel_id=1, source_target_pairs={{0,16},{16,0},{1,17},{17,1},{2,18},{18,2},{3,19},{19,3},{4,20},{20... | collective-permute-start | bytes 2949128 | tf_op jit(solution)/shard_map/ppermute | solution.py:302
  57.2 2.2 %collective-permute-done.sib_ref = bf16[4,192,640]{2,1,0:T(8,128)(2,1)S(1)} collective-permute-done((bf16[4,192,640]{2,1,0:T(8,128)(2,1)S(1)}, bf16[4,192,640]{2,1,0:T(8,128)(2,1)S(1)}, u32[]{:S(2)}, u32[]{:S(2)}) %collective-permute-start) | collective-permute-done | bytes 983072 | tf_op jit(solution)/shard_map/ppermute | solution.py:302
  59.4 0.0 copy-done
  59.4 0.0 copy-done.1
  59.4 2.9 %shard_map.78 = (bf16[512,1280]{1,0:T(8,128)(2,1)S(1)}, f32[256,512]{1,0:T(8,128)S(1)}, f32[256,512]{1,0:T(8,128)S(1)}, f32[256,512]{1,0:T(8,128)S(1)}, f32[256,...) custom-call(bf16[4,192,640]{2,1,0:T(8,128)(2,1)S(1)} %all_to_all.21., ...), custom_call_target="tpu_custom_call" | custom-call | tf_op jit(solution)/shard_map/pallas_call | solution.py:287
  62.3 2.3 %collective-permute-start.1 = (bf16[528,1280]{1,0:T(8,128)(2,1)S(1)}, bf16[528,1280]{1,0:T(8,128)(2,1)S(1)}, u32[]{:S(2)}, u32[]{:S(2)}) collective-permute-start(bf16[528,1280]{1,0:T(8,128)(2,1)S(1)} %get-tuple-element.13), channel_id=1, source_target_pairs={{0,16},{16,0},{1,17},{17,1},{2,18},{18,2},{3,19},{19,3},{4,20},{20... | collective-permute-start | bytes 4055048 | tf_op jit(solution)/shard_map/ppermute | solution.py:302
  64.6 2.7 %collective-permute-done.1.got_ref = bf16[528,1280]{1,0:T(8,128)(2,1)S(1)} collective-permute-done((bf16[528,1280]{1,0:T(8,128)(2,1)S(1)}, bf16[528,1280]{1,0:T(8,128)(2,1)S(1)}, u32[]{:S(2)}, u32[]{:S(2)}) %collective-permute-start.1) | collective-permute-done | bytes 1351712 | tf_op jit(solution)/shard_map/ppermute | solution.py:302
  67.3 0.8 shard_map.79
  68.1 20.7 %all_to_all.22.got_ref = bf16[4,272,640]{2,1,0:T(8,128)(2,1)S(1)} all-to-all(bf16[4,272,640]{2,1,0:T(8,128)(2,1)S(1)} %shard_map.79), channel_id=1, replica_groups=mesh['xh'=2,'z'=8,'core'=2,'y'=8,'xl'=2] {'xh','xl'}, dimensions={0} | all-to-all | bytes 2785280 | tf_op jit(solution)/shard_map/all_to_all | solution.py:319
  88.8 0.6 shard_map.80
  89.4 25.9 %all_to_all.23.got_ref = bf16[128,8,256]{2,1,0:T(8,128)(2,1)S(1)} all-to-all(bf16[128,8,256]{2,1,0:T(8,128)(2,1)S(1)} %shard_map.80), channel_id=1, replica_groups=mesh['xh'=2,'z'=8,'core'=2,'y'=8,'xl'=2] {'z','core','y'}, dimensions={0} | all-to-all | bytes 1048576 | tf_op jit(solution)/shard_map/all_to_all | solution.py:321
  115.3 2.7 %shard_map.81 = (bf16[512,1280]{1,0:T(8,128)(2,1)}, f32[16,40]{1,0:T(8,128)}, f32[16,40]{1,0:T(8,128)}) custom-call(bf16[128,8,256]{2,1,0:T(8,128)(2,1)S(1)} %all_to_all.23.got_ref, bf16[512,1280]{1,0:T(8,128)(2,1)S(1)} %get-tuple-element.15.g_ref, f32[256,512]{1,0:T(8,128)S(1)} %get-tuple-element.16.e_ref, f32[256,512]{1,0:T(8,128)S(1)} %get-tuple-element.17.part_ref, ...), custom_call_target="tpu_custom_call" | custom-call | tf_op jit(solution)/shard_map/pallas_call | solution.py:287
Async XLA Ops:
  0.6 0.7 copy-start.2
  1.3 0.7 copy-start.3
  2.0 0.7 copy-start.4
  35.7 23.6 %copy-start = (bf16[512,1280]{1,0:T(8,128)(2,1)S(1)}, bf16[512,1280]{1,0:T(8,128)(2,1)}, u32[]{:S(2)}) copy-start(bf16[512,1280]{1,0:T(8,128)(2,1)} %tok_ref.1) | copy-start | bytes 3932164
  35.7 23.6 %copy-start.1 = (bf16[512,1280]{1,0:T(8,128)(2,1)S(1)}, bf16[512,1280]{1,0:T(8,128)(2,1)}, u32[]{:S(2)}) copy-start(bf16[512,1280]{1,0:T(8,128)(2,1)} %og_ref.1) | copy-start | bytes 3932164
  53.8 5.6 %collective-permute-start = (bf16[4,192,640]{2,1,0:T(8,128)(2,1)S(1)}, bf16[4,192,640]{2,1,0:T(8,128)(2,1)S(1)}, u32[]{:S(2)}, u32[]{:S(2)}) collective-permute-start(bf16[4,192,640]{2,1,0:T(8,128)(2,1)S(1)} %all_to_all.21.own_ref), channel_id=1, source_target_pairs={{0,16},{16,0},{1,17},{17,1},{2,18},{18,2},{3,19},{19,3},{4,20},{20... | collective-permute-start | bytes 2949128 | tf_op jit(solution)/shard_map/ppermute | solution.py:302
  62.3 5.0 %collective-permute-start.1 = (bf16[528,1280]{1,0:T(8,128)(2,1)S(1)}, bf16[528,1280]{1,0:T(8,128)(2,1)S(1)}, u32[]{:S(2)}, u32[]{:S(2)}) collective-permute-start(bf16[528,1280]{1,0:T(8,128)(2,1)S(1)} %get-tuple-element.13), channel_id=1, source_target_pairs={{0,16},{16,0},{1,17},{17,1},{2,18},{18,2},{3,19},{19,3},{4,20},{20... | collective-permute-start | bytes 4055048 | tf_op jit(solution)/shard_map/ppermute | solution.py:302

commit v3 on v2

--- a/solution.py
+++ b/solution.py
@@ -11,7 +11,7 @@
 X = ("xh", "xl")
 LANES = 128
 WIDE = 40
-VMEM_BYTES = 32 * 1024 * 1024
+VMEM_BYTES = 16 * 1024 * 1024
 
 
 def nt(a, b):
@@ -70,13 +70,19 @@
     return f[:, :LANES] + f[:, LANES:2 * LANES] + f[:, 2 * LANES:3 * LANES]
 
 
-def pieces_kernel(e_ref, o_ref, i_ref, out_ref):
-    def at(ref, k):
-        x = ref[...].astype(F32)
+def pieces_kernel(e_ref, o_ref, i_ref, out_ref, in_ref, sems):
+    copies = [pltpu.make_async_copy(ref, in_ref.at[k], sems.at[k]) for k, ref in enumerate((e_ref, o_ref, i_ref))]
+    for copy in copies:
+        copy.start()
+    for copy in copies:
+        copy.wait()
+
+    def at(k):
+        x = in_ref[k].astype(F32)
         x = jnp.concatenate([x, jnp.zeros((16, LANES - WIDE), F32)], axis=1)
         return roll(x, k * WIDE)
 
-    x = at(e_ref, 0) + at(o_ref, 1) + at(i_ref, 2)
+    x = at(0) + at(1) + at(2)
     for half in range(2):
         rows = x[half * 8:half * 8 + 8]
         many = jnp.broadcast_to(rows[None], (8, 8, LANES)).astype(BF)
@@ -101,44 +107,79 @@
             out_ref[j, a * 64:(a + 1) * 64, :] = whole
 
 
-def main_kernel(own_ref, sib_ref, tok_ref, og_ref,
-                g_ref, e_ref, part_ref, dc_ref, m_ref, t_ref, p_ref, down_ref, dsib_ref, outs_ref):
-    for h, ref in ((0, own_ref), (1, sib_ref)):
-        for xl in range(2):
-            for xh in range(2):
-                rows = pl.ds(h * 128 + xl * 64, 64)
-                cols = pl.ds(xh * 640, 640)
-                j = xh * 2 + xl
-                g_ref[rows, cols] = ref[j, 0:64, :]
-                outs_ref[rows, cols] = ref[j, 64:128, :]
-                g_ref[pl.ds(256 + h * 128 + xl * 64, 64), cols] = ref[j, 128:192, :]
-    tok = tok_ref[...]
-    og = og_ref[...]
-    cgrad = nt(outs_ref[...], og)
-    logits = nt(g_ref[0:256, :], tok)
-    dgrad = nt(g_ref[256:512, :], tok)
-    raised = jnp.exp(logits - jnp.max(logits, axis=0, keepdims=True))
-    combine = raised / jnp.sum(raised, axis=0, keepdims=True)
-    row = jnp.sum(combine * cgrad, axis=0, keepdims=True)
-    part = combine * (cgrad - row)
+def scores_kernel(got_ref, tok_ref, tok2_ref, og_ref, og2_ref, g_ref, lg_ref, dg_ref, cg_ref, r_ref, outs_ref):
+    for xl in range(2):
+        for xh in range(2):
+            at, cols, j = xl * 64, pl.ds(xh * 640, 640), xh * 2 + xl
+            g_ref[at:at + 64, cols] = got_ref[j, 0:64, :]
+            outs_ref[at:at + 64, cols] = got_ref[j, 64:128, :]
+            g_ref[128 + at:192 + at, cols] = got_ref[j, 128:192, :]
+    g = g_ref[...]
+    outs = outs_ref[...]
+    r_ref[...] = jnp.zeros_like(r_ref)
+    for h, (tok, og) in enumerate(((tok_ref, og_ref), (tok2_ref, og2_ref))):
+        cols = pl.ds(h * 512, 512)
+        both = nt(g, tok[...])
+        cgrad = nt(outs, og[...])
+        logits = both[:128]
+        lg_ref[:, cols] = logits
+        dg_ref[:, cols] = both[128:]
+        cg_ref[:, cols] = cgrad
+        top = jnp.max(logits, axis=0, keepdims=True)
+        raised = jnp.exp(logits - top)
+        r_ref[0:1, cols] = top
+        r_ref[1:2, cols] = jnp.sum(raised, axis=0, keepdims=True)
+        r_ref[2:3, cols] = jnp.sum(raised * cgrad, axis=0, keepdims=True)
+
+
+def slots_kernel(lg_ref, dg_ref, tok_ref, tok2_ref, e_ref, dc_ref, p_ref, bc_ref):
+    logits = lg_ref[...]
+    dgrad = dg_ref[...]
     m = jnp.max(logits, axis=1, keepdims=True)
     e = jnp.exp(logits - m)
     s = jnp.sum(e, axis=1, keepdims=True)
     t = jnp.sum(e * dgrad, axis=1, keepdims=True) / s
     dc = dgrad - t
     e_ref[...] = e
-    part_ref[...] = part
     dc_ref[...] = dc
-    m_ref[...] = m
-    t_ref[...] = t
-    p = packed(m, 32, 0) + packed(s, 32, 32) + packed(t, 32, 64)
-    p_ref[...] = p
-    for k, (left, right) in enumerate(((combine, og), (part, tok), (e * dc, tok), (e, tok))):
-        x = nn(left.astype(BF), right).astype(BF)
-        down_ref[k * 128:(k + 1) * 128, :] = x[:128]
-        dsib_ref[k * 128:(k + 1) * 128, :] = x[128:]
-    dsib_ref[512:528, 0:640] = stat_rows(p)
-    dsib_ref[512:528, 640:1280] = jnp.zeros((16, 640), BF)
+    p_ref[...] = packed(m, 16, 0) + packed(s, 16, 16) + packed(t, 16, 32)
+    left = jnp.concatenate([(e * dc).astype(BF), e.astype(BF)], axis=0)
+    bc_ref[...] = (nn(left[:, :512], tok_ref[...]) + nn(left[:, 512:], tok2_ref[...])).astype(BF)
+
+
+def tokens_kernel(lg_ref, cg_ref, r_ref, r2_ref, e_ref, dc_ref, p_ref, bc_ref, tok_ref, tok2_ref, og_ref, og2_ref,
+                  out_ref, keep_ref, send_ref):
+    def put(k, x):
+        for xh in range(2):
+            for xl in range(2):
+                out_ref[xh * 2 + xl, k * 64:(k + 1) * 64, :] = x[xl * 64:(xl + 1) * 64, xh * 640:(xh + 1) * 640]
+
+    o = a = None
+    for h, (tok, og, keep) in enumerate(((tok_ref, og_ref, keep_ref), (tok2_ref, og2_ref, send_ref))):
+        cols = pl.ds(h * 512, 512)
+        other = pl.ds((1 - h) * 512, 512)
+        m1, m2 = r_ref[0:1, cols], r2_ref[0:1, other]
+        top = jnp.maximum(m1, m2)
+        w1, w2 = jnp.exp(m1 - top), jnp.exp(m2 - top)
+        total = w1 * r_ref[1:2, cols] + w2 * r2_ref[1:2, other]
+        row = (w1 * r_ref[2:3, cols] + w2 * r2_ref[2:3, other]) / total
+        combine = jnp.exp(lg_ref[:, cols] - top) / total
+        part = combine * (cg_ref[:, cols] - row)
+        keep[0:128, :] = e_ref[:, cols]
+        keep[128:256, :] = part
+        keep[256:384, :] = dc_ref[:, cols]
+        keep[384:392, 0:LANES] = p_ref[...]
+        keep[384:392, LANES:512] = jnp.zeros((8, 512 - LANES), F32)
+        o1 = nn(combine.astype(BF), og[...])
+        a1 = nn(part.astype(BF), tok[...])
+        o, a = (o1, a1) if h == 0 else (o + o1, a + a1)
+    put(0, o.astype(BF))
+    put(1, a.astype(BF))
+    put(2, bc_ref[0:128, :])
+    put(3, bc_ref[128:256, :])
+    stats = stat_rows(p_ref[...])
+    for j in range(4):
+        out_ref[j, 256:272, :] = stats
 
 
 def merge_stats(ps, groups, exact=True):
@@ -163,38 +204,9 @@
     return top, total, mean, ws, [t - mean for t in ts]
 
 
-def core_kernel(own_ref, got_ref, p_ref, out_ref):
-    lane = lane_of((8, LANES))
-    q = stat_read(got_ref[512:528, 0:640])
-    q = jnp.where(lane % 32 < 16, roll(q, -16), roll(q, 16))
-    top, total, mean, ws, ds = merge_stats([p_ref[...], q], 32)
-    ok = lane < 32
-    p = jnp.where(ok, top, 0.0) + roll(jnp.where(ok, total, 0.0), 32) + roll(jnp.where(ok, mean, 0.0), 64)
-    stats = stat_rows(p)
-    w1, w2 = columns(ws[0], 16, 0), columns(ws[1], 16, 0)
-    d1, d2 = columns(ds[0], 16, 0), columns(ds[1], 16, 0)
-
-    def rows(ref, k):
-        return ref[k * 128:(k + 1) * 128, :].astype(F32)
-
-    def put(k, x):
-        x = x.astype(BF)
-        for xh in range(2):
-            for xl in range(2):
-                out_ref[xh * 2 + xl, k * 64:(k + 1) * 64, :] = x[xl * 64:(xl + 1) * 64, xh * 640:(xh + 1) * 640]
-
-    put(0, rows(own_ref, 0) + rows(got_ref, 0))
-    put(1, rows(own_ref, 1) + rows(got_ref, 1))
-    c1, c2 = w1 * rows(own_ref, 3), w2 * rows(got_ref, 3)
-    put(2, w1 * rows(own_ref, 2) + w2 * rows(got_ref, 2) + d1 * c1 + d2 * c2)
-    put(3, c1 + c2)
-    for j in range(4):
-        out_ref[j, 256:272, :] = stats
-
-
 def x_kernel(got_ref, out_ref):
     xl = lax.axis_index("xl")
-    top, total, mean, ws, ds = merge_stats([stat_read(got_ref[j, 256:272, :]) for j in range(4)], 32, False)
+    top, total, mean, ws, ds = merge_stats([stat_read(got_ref[j, 256:272, :]) for j in range(4)], 16, False)
     ws = [columns(w, 8, xl * 8) for w in ws]
     ds = [columns(d, 8, xl * 8) for d in ds]
 
@@ -229,7 +241,7 @@
         out_ref[k * 8:(k + 1) * 8, :, LANES:2 * LANES] = high.reshape(8, 8, LANES).astype(BF)
 
 
-def last_kernel(got_ref, g_ref, e_ref, part_ref, dc_ref, m_ref, t_ref, tg_ref, eg_ref, og_ref, l_ref):
+def last_kernel(got_ref, g_ref, g2_ref, keep_ref, keep2_ref, tg_ref, eg_ref, og_ref):
     xl, y, core = lax.axis_index("xl"), lax.axis_index("y"), lax.axis_index("core")
     big = (8, 2, 8, 8, LANES)
     t0 = got_ref[:, :, 0:LANES].astype(F32).reshape(big)
@@ -266,19 +278,22 @@
         eg_ref[c * 8:(c + 1) * 8, :] = grad[:, 0:WIDE]
         og_ref[c * 8:(c + 1) * 8, :] = q[:, 0:WIDE]
 
-    for h in range(2):
+    total_grad = None
+    for h, (gr, kr) in enumerate(((g_ref, keep_ref), (g2_ref, keep2_ref))):
         second = (core + h) == 1
 
         def cols(v):
             return columns(jnp.where(second, v[1], v[0]), 16, 32)
 
-        at = pl.ds(h * 128, 128)
-        alpha = jnp.exp(m_ref[at, :] - cols(top)) / cols(total)
-        shift = t_ref[at, :] - cols(mean)
-        disp = e_ref[at, :] * alpha
-        l_ref[at, :] = (part_ref[at, :] + disp * (dc_ref[at, :] + shift)).astype(BF)
-        l_ref[pl.ds(256 + h * 128, 128), :] = disp.astype(BF)
-    tg_ref[...] = tn(l_ref[...], g_ref[...]).astype(BF)
+        q = kr[384:392, 0:LANES]
+        alpha = jnp.exp(columns(q, 16, 0) - cols(top)) / cols(total)
+        shift = columns(q, 16, 32) - cols(mean)
+        disp = kr[0:128, :] * alpha
+        grad = kr[128:256, :] + disp * (kr[256:384, :] + shift)
+        left = jnp.concatenate([grad.astype(BF), disp.astype(BF)], axis=0)
+        x = tn(left, gr[...])
+        total_grad = x if h == 0 else total_grad + x
+    tg_ref[...] = total_grad.astype(BF)
 
 
 def call(kernel, outs, *args, scratch=(), flops=0):
@@ -303,27 +318,40 @@
 
 
 def per_device(tokens, slot_embed, slot_outputs, output_grad, slot_input_grad):
-    op = call(pieces_kernel, shape(128, 8, LANES), slot_embed, slot_outputs, slot_input_grad)
+    f32 = jnp.float32
+    op = pl.pallas_call(
+        pieces_kernel,
+        out_shape=shape(128, 8, LANES),
+        in_specs=[pl.BlockSpec(memory_space=pl.ANY)] * 3,
+        out_specs=pl.BlockSpec(memory_space=pltpu.VMEM),
+        scratch_shapes=[pltpu.VMEM((3, 16, WIDE), BF), pltpu.SemaphoreType.DMA((3,))],
+        compiler_params=pltpu.CompilerParams(vmem_limit_bytes=60 * 1024 * 1024),
+    )(slot_embed, slot_outputs, slot_input_grad)
+    op, tok1 = lax.optimization_barrier((op, tokens))
+    tok2 = swap(tok1)
     got = lax.all_to_all(op, YZ, 0, 0, tiled=True)
     op = call(widen_kernel, shape(4, 192, 640), got)
-    own = lax.all_to_all(op, X, 0, 0, tiled=True)
-    sib = swap(own)
-    g, e, part, dc, m, t, p, down, dsib = call(
-        main_kernel,
-        [shape(512, 1280), shape(256, 512, dtype=F32), shape(256, 512, dtype=F32), shape(256, 512, dtype=F32),
-         shape(256, 1, dtype=F32), shape(256, 1, dtype=F32), shape(8, LANES, dtype=F32),
-         shape(512, 1280), shape(528, 1280)],
-        own, sib, tokens, output_grad,
-        scratch=[pltpu.VMEM((256, 1280), BF)])
-    op = call(core_kernel, shape(4, 272, 640), down, swap(dsib), p)
+    op, og1 = lax.optimization_barrier((op, output_grad))
+    og2 = swap(og1)
     got = lax.all_to_all(op, X, 0, 0, tiled=True)
+    wide = shape(128, 1024, dtype=f32)
+    g, lg, dg, cg, r = call(
+        scores_kernel, [shape(256, 1280), wide, wide, wide, shape(8, 1024, dtype=f32)],
+        got, tokens, tok2, output_grad, og2, scratch=[pltpu.VMEM((128, 1280), BF)])
+    r2 = swap(r)
+    e, dc, p, bc = call(
+        slots_kernel, [wide, wide, shape(8, LANES, dtype=f32), shape(256, 1280)], lg, dg, tokens, tok2)
+    op, keep, send = call(
+        tokens_kernel, [shape(4, 272, 640), shape(392, 512, dtype=f32), shape(392, 512, dtype=f32)],
+        lg, cg, r, r2, e, dc, p, bc, tokens, tok2, output_grad, og2)
+    got = lax.all_to_all(op, X, 0, 0, tiled=True)
+    g2, keep2 = swap(g), swap(send)
     op = call(x_kernel, shape(128, 8, 2 * LANES), got)
     got = lax.all_to_all(op, YZ, 0, 0, tiled=True)
     return call(
         last_kernel,
-        [shape(512, 1280), shape(16, WIDE, dtype=F32), shape(16, WIDE, dtype=F32)],
-        got, g, e, part, dc, m, t,
-        scratch=[pltpu.VMEM((512, 512), BF)])
+        [shape(512, 1280), shape(16, WIDE, dtype=f32), shape(16, WIDE, dtype=f32)],
+        got, g, g2, keep, keep2)
 
 
 def solution(mesh):

time: 118 us -> 116 us (0.983)
  blocking collectives: 97.3 us -> 38.9 us
  starting transfers between devices: 5.71 us -> 38.2 us
  waiting for transfers between devices: 4.87 us -> 25.6 us
  Pallas kernels: 7.35 us -> 9.49 us
    all_to_all x3 -> x0, blocking collectives: 76.6 us -> none  [the longest x2 58.8 us: per_device(): got = lax.all_to_all(op, YZ, 0, 0, tiled=True)]
    all_to_all x0 -> x2, starting transfers between devices: none -> 24.8 us  [per_device(): got = lax.all_to_all(op, YZ, 0, 0, tiled=True)]
    all_to_all x0 -> x2, waiting for transfers between devices: none -> 23.5 us  [per_device(): got = lax.all_to_all(op, YZ, 0, 0, tiled=True)]
    all_to_all x1 -> x2, blocking collectives: 20.7 us -> 38.9 us  [per_device(): got = lax.all_to_all(op, X, 0, 0, tiled=True)]
    ppermute x2 -> x5, starting transfers between devices: 5.71 us -> 13.4 us  [swap(): return lax.ppermute(x, 'core', [(0, 1), (1, 0)])]
    ppermute x2 -> x5, waiting for transfers between devices: 4.87 us -> 2.07 us  [swap(): return lax.ppermute(x, 'core', [(0, 1), (1, 0)])]
    pallas_call x0 -> x1, Pallas kernels: none -> 1.54 us  [per_device(): pl.pallas_call(pieces_kernel, out_shape=shape(128, 8, LANES), in_specs=[p...]
  transfers between devices with their start and end apart: 2 -> 7, of which waited for: 2 -> 3; matrix products, arithmetic and copies ran while one was open for 0% -> 0% of each run, Pallas kernels for 0% -> 1%
where the time goes in v3:
time: 116 us; the launch traced here: 115 us
  blocking collectives  38.9 us (34%)
  starting transfers between devices  38.2 us (33%)
  waiting for transfers between devices  25.6 us (22%)
  Pallas kernels  9.49 us (8%)
  local copies, waits for them, and re-layouts  1.95 us (2%)
    all_to_all x2, blocking collectives, per_device(): got = lax.all_to_all(op, X, 0, 0, tiled=True)  38.9 us
    all_to_all x2, starting transfers between devices, per_device(): got = lax.all_to_all(op, YZ, 0, 0, tiled=True)  24.8 us
    all_to_all x2, waiting for transfers between devices, per_device(): got = lax.all_to_all(op, YZ, 0, 0, tiled=True)  23.5 us
    ppermute x5, starting transfers between devices, swap(): return lax.ppermute(x, 'core', [(0, 1), (1, 0)])  13.4 us
    pallas_call x6, Pallas kernels, call(): pl.pallas_call(kernel, out_shape=outs, in_specs=[vm] * len(args), out_spe...  7.95 us
  transfers between devices with their start and end apart: 7, of which 3 were waited for; matrix products, arithmetic and copies ran while one was open for 0% of the time, Pallas kernels for 1%

profile of v3, /device:TPU:1, one launch (start us, length us, event | category | flops | bytes accessed | tf_op | source)
XLA Modules:
  0.0 115.0 jit_solution(13702148264296939636)
XLA Ops:
  0.6 1.5 %shard_map.76 = bf16[128,8,128]{2,1,0:T(8,128)(2,1)} custom-call(bf16[16,40]{1,0:T(8,128)(2,1)} %e_ref.1, bf16[16,40]{1,0:T(8,128)(2,1)} %o_ref.1, bf16[16,40]{1,0:T(8,128)(2,1)} %i_ref.1), custom_call_target="tpu_custom_call" | custom-call | tf_op jit(solution)/shard_map/pallas_call | solution.py:322
  2.2 18.4 %all-to-all-start = ((bf16[128,8,128]{2,1,0:T(8,128)(2,1)}), bf16[128,8,128]{2,1,0:T(8,128)(2,1)S(1)}, u32[]{:S(2)}, u32[]{:S(2)}) async-start(bf16[128,8,128]{2,1,0:T(8,128)(2,1)} %shard_map.76), calls=%async_computation | async-start | bytes 524288 | tf_op jit(solution)/shard_map/all_to_all | solution.py:332
  20.6 0.0 copy-start
  20.6 2.9 %collective-permute-start = (bf16[512,1280]{1,0:T(8,128)(2,1)}, bf16[512,1280]{1,0:T(8,128)(2,1)S(1)}, u32[]{:S(2)}, u32[]{:S(2)}) collective-permute-start(bf16[512,1280]{1,0:T(8,128)(2,1)} %tok_ref.5), channel_id=1, source_target_pairs={{0,16},{16,0},{1,17},{17,1},{2,18},{18,2},{3,19},{19,3},{4,20},{20... | collective-permute-start | bytes 3932168 | tf_op jit(solution)/shard_map/ppermute | solution.py:317
  23.6 11.8 %all-to-all-done.got_ref = bf16[128,8,128]{2,1,0:T(8,128)(2,1)S(1)} async-done(((bf16[128,8,128]{2,1,0:T(8,128)(2,1)}), bf16[128,8,128]{2,1,0:T(8,128)(2,1)S(1)}, u32[]{:S(2)}, u32[]{:S(2)}) %all-to-all-start) | async-done | bytes 262176 | tf_op jit(solution)/shard_map/all_to_all | solution.py:332
  35.3 0.3 shard_map.77
  35.6 2.3 %collective-permute-start.1 = (bf16[512,1280]{1,0:T(8,128)(2,1)}, bf16[512,1280]{1,0:T(8,128)(2,1)S(1)}, u32[]{:S(2)}, u32[]{:S(2)}) collective-permute-start(bf16[512,1280]{1,0:T(8,128)(2,1)} %og_ref.3), channel_id=1, source_target_pairs={{0,16},{16,0},{1,17},{17,1},{2,18},{18,2},{3,19},{19,3},{4,20},{20... | collective-permute-start | bytes 3932168 | tf_op jit(solution)/shard_map/ppermute | solution.py:317
  37.9 17.6 %all_to_all.20.got_ref = bf16[4,192,640]{2,1,0:T(8,128)(2,1)S(1)} all-to-all(bf16[4,192,640]{2,1,0:T(8,128)(2,1)S(1)} %shard_map.77), channel_id=1, replica_groups=mesh['xh'=2,'z'=8,'core'=2,'y'=8,'xl'=2] {'xh','xl'}, dimensions={0} | all-to-all | bytes 1966080 | tf_op jit(solution)/shard_map/all_to_all | solution.py:336
  55.6 0.0 collective-permute-done.tok2_ref
  55.6 0.0 collective-permute-done.1.og2_ref
  55.6 0.0 copy-done
  55.6 0.0 copy-done.1
  55.6 1.7 %shard_map.78 = (bf16[256,1280]{1,0:T(8,128)(2,1)S(1)}, f32[128,1024]{1,0:T(8,128)S(1)}, f32[128,1024]{1,0:T(8,128)S(1)}, f32[128,1024]{1,0:T(8,128)S(1)}, f32[8,1024]{1,0:T(8,128)S(1)}) custom-call(bf16[4,192,640]{2,1,0:T(8,128)(2,1)S(1)} %all_to_all.20.got_ref, bf16[512,1280]{1,0:T(8,128)(2,1)S(1)} %copy-done, ...), custom_call_target="tpu_custom_call" | custom-call | tf_op jit(solution)/shard_map/pallas_call | solution.py:302
  57.3 0.0 copy-start.2
  57.3 3.4 %collective-permute-start.2 = (f32[8,1024]{1,0:T(8,128)S(1)}, f32[8,1024]{1,0:T(8,128)S(1)}, u32[]{:S(2)}, u32[]{:S(2)}) collective-permute-start(f32[8,1024]{1,0:T(8,128)S(1)} %get-tuple-element.25.r_ref), channel_id=1, source_target_pairs={{0,16},{16,0},{1,17},{17,1},{2,18},{18,2},{3,19},{19,3},{4,20},{20... | collective-permute-start | bytes 98312 | tf_op jit(solution)/shard_map/ppermute | solution.py:317
  60.7 1.1 shard_map.79
  61.8 0.0 copy-done.2
  61.8 0.0 collective-permute-done.2.r2_ref
  61.9 1.0 shard_map.80
  62.8 0.0 copy-start.6
  62.8 21.3 %all_to_all.21.got_ref = bf16[4,272,640]{2,1,0:T(8,128)(2,1)S(1)} all-to-all(bf16[4,272,640]{2,1,0:T(8,128)(2,1)S(1)} %get-tuple-element.31), channel_id=1, replica_groups=mesh['xh'=2,'z'=8,'core'=2,'y'=8,'xl'=2] {'xh','xl'}, dimensions={0} | all-to-all | bytes 2785280 | tf_op jit(solution)/shard_map/all_to_all | solution.py:347
  84.1 0.0 copy-done.6
  84.1 1.4 %shard_map.81 = bf16[128,8,256]{2,1,0:T(8,128)(2,1)} custom-call(bf16[4,272,640]{2,1,0:T(8,128)(2,1)S(1)} %all_to_all.21.got_ref), custom_call_target="tpu_custom_call" | custom-call | tf_op jit(solution)/shard_map/pallas_call | solution.py:302
  85.6 6.4 %all-to-all-start.3 = ((bf16[128,8,256]{2,1,0:T(8,128)(2,1)}), bf16[128,8,256]{2,1,0:T(8,128)(2,1)S(1)}, u32[]{:S(2)}, u32[]{:S(2)}) async-start(bf16[128,8,256]{2,1,0:T(8,128)(2,1)} %shard_map.81), calls=%async_computation.3 | async-start | bytes 1048576 | tf_op jit(solution)/shard_map/all_to_all | solution.py:350
  92.0 2.8 %collective-permute-start.4 = (f32[392,512]{1,0:T(8,128)}, f32[392,512]{1,0:T(8,128)S(1)}, u32[]{:S(2)}, u32[]{:S(2)}) collective-permute-start(f32[392,512]{1,0:T(8,128)} %copy-done.6), channel_id=1, source_target_pairs={{0,16},{16,0},{1,17},{17,1},{2,18},{18,2},{3,19},{19,3},{4,20},{20... | collective-permute-start | bytes 2408456 | tf_op jit(solution)/shard_map/ppermute | solution.py:317
  94.8 1.9 %collective-permute-start.3 = (bf16[256,1280]{1,0:T(8,128)(2,1)S(1)}, bf16[256,1280]{1,0:T(8,128)(2,1)S(1)}, u32[]{:S(2)}, u32[]{:S(2)}) collective-permute-start(bf16[256,1280]{1,0:T(8,128)(2,1)S(1)} %copy-done.3), channel_id=1, source_target_pairs={{0,16},{16,0},{1,17},{17,1},{2,18},{18,2},{3,19},{19,3},{4,20},{20... | collective-permute-start | bytes 1966088 | tf_op jit(solution)/shard_map/ppermute | solution.py:317
  96.7 2.1 %collective-permute-done.3.g2_ref = bf16[256,1280]{1,0:T(8,128)(2,1)S(1)} collective-permute-done((bf16[256,1280]{1,0:T(8,128)(2,1)S(1)}, bf16[256,1280]{1,0:T(8,128)(2,1)S(1)}, u32[]{:S(2)}, u32[]{:S(2)}) %collective-permute-start.3) | collective-permute-done | bytes 655392 | tf_op jit(solution)/shard_map/ppermute | solution.py:317
  98.8 0.8 copy-done.4
  99.6 0.0 collective-permute-done.4.keep2_ref
  99.6 11.8 %all-to-all-done.3.got_ref = bf16[128,8,256]{2,1,0:T(8,128)(2,1)S(1)} async-done(((bf16[128,8,256]{2,1,0:T(8,128)(2,1)}), bf16[128,8,256]{2,1,0:T(8,128)(2,1)S(1)}, u32[]{:S(2)}, u32[]{:S(2)}) %all-to-all-start.3) | async-done | bytes 524320 | tf_op jit(solution)/shard_map/all_to_all | solution.py:350
  111.4 1.1 copy-done.5
  112.5 2.5 %shard_map.82 = (bf16[512,1280]{1,0:T(8,128)(2,1)}, f32[16,40]{1,0:T(8,128)}, f32[16,40]{1,0:T(8,128)}) custom-call(bf16[128,8,256]{2,1,0:T(8,128)(2,1)S(1)} %all-to-all-done.3.got_ref, bf16[256,1280]{1,0:T(8,128)(2,1)S(1)} %copy-done.3, bf16[256,1280]{1,0:T(8,128)(2,1)S(1)} %copy-done.5, f32[392,512]{1,0:T(8,128)S(1)} %get-tuple-element.33.keep_ref, ...), custom_call_target="tpu_custom_call" | custom-call | tf_op jit(solution)/shard_map/pallas_call | solution.py:302
  (5 shorter events, 0.0 us)
Async XLA Ops:
  2.2 33.2 %all-to-all-start = ((bf16[128,8,128]{2,1,0:T(8,128)(2,1)}), bf16[128,8,128]{2,1,0:T(8,128)(2,1)S(1)}, u32[]{:S(2)}, u32[]{:S(2)}) async-start(bf16[128,8,128]{2,1,0:T(8,128)(2,1)} %shard_map.76), calls=%async_computation | async-start | bytes 524288 | tf_op jit(solution)/shard_map/all_to_all | solution.py:332
  20.6 35.0 %copy-start = (bf16[512,1280]{1,0:T(8,128)(2,1)S(1)}, bf16[512,1280]{1,0:T(8,128)(2,1)}, u32[]{:S(2)}) copy-start(bf16[512,1280]{1,0:T(8,128)(2,1)} %tok_ref.5) | copy-start | bytes 3932164
  20.6 34.9 %collective-permute-start = (bf16[512,1280]{1,0:T(8,128)(2,1)}, bf16[512,1280]{1,0:T(8,128)(2,1)S(1)}, u32[]{:S(2)}, u32[]{:S(2)}) collective-permute-start(bf16[512,1280]{1,0:T(8,128)(2,1)} %tok_ref.5), channel_id=1, source_target_pairs={{0,16},{16,0},{1,17},{17,1},{2,18},{18,2},{3,19},{19,3},{4,20},{20... | collective-permute-start | bytes 3932168 | tf_op jit(solution)/shard_map/ppermute | solution.py:317
  35.3 20.2 %copy-start.1 = (bf16[512,1280]{1,0:T(8,128)(2,1)S(1)}, bf16[512,1280]{1,0:T(8,128)(2,1)}, u32[]{:S(2)}) copy-start(bf16[512,1280]{1,0:T(8,128)(2,1)} %og_ref.3) | copy-start | bytes 3932164
  35.6 20.0 %collective-permute-start.1 = (bf16[512,1280]{1,0:T(8,128)(2,1)}, bf16[512,1280]{1,0:T(8,128)(2,1)S(1)}, u32[]{:S(2)}, u32[]{:S(2)}) collective-permute-start(bf16[512,1280]{1,0:T(8,128)(2,1)} %og_ref.3), channel_id=1, source_target_pairs={{0,16},{16,0},{1,17},{17,1},{2,18},{18,2},{3,19},{19,3},{4,20},{20... | collective-permute-start | bytes 3932168 | tf_op jit(solution)/shard_map/ppermute | solution.py:317
  57.3 4.5 %copy-start.2 = (bf16[256,1280]{1,0:T(8,128)(2,1)}, bf16[256,1280]{1,0:T(8,128)(2,1)S(1)}, u32[]{:S(2)}) copy-start(bf16[256,1280]{1,0:T(8,128)(2,1)S(1)} %get-tuple-element.32.g_ref) | copy-start | bytes 1966084
  57.3 4.5 %collective-permute-start.2 = (f32[8,1024]{1,0:T(8,128)S(1)}, f32[8,1024]{1,0:T(8,128)S(1)}, u32[]{:S(2)}, u32[]{:S(2)}) collective-permute-start(f32[8,1024]{1,0:T(8,128)S(1)} %get-tuple-element.25.r_ref), channel_id=1, source_target_pairs={{0,16},{16,0},{1,17},{17,1},{2,18},{18,2},{3,19},{19,3},{4,20},{20... | collective-permute-start | bytes 98312 | tf_op jit(solution)/shard_map/ppermute | solution.py:317
  62.8 21.3 %copy-start.6 = (f32[392,512]{1,0:T(8,128)}, f32[392,512]{1,0:T(8,128)S(1)}, u32[]{:S(2)}) copy-start(f32[392,512]{1,0:T(8,128)S(1)} %get-tuple-element.34) | copy-start | bytes 2408452
  84.1 10.6 %copy-start.3 = (bf16[256,1280]{1,0:T(8,128)(2,1)S(1)}, bf16[256,1280]{1,0:T(8,128)(2,1)}, u32[]{:S(2)}) copy-start(bf16[256,1280]{1,0:T(8,128)(2,1)} %copy-done.2) | copy-start | bytes 1966084
  85.6 25.8 %all-to-all-start.3 = ((bf16[128,8,256]{2,1,0:T(8,128)(2,1)}), bf16[128,8,256]{2,1,0:T(8,128)(2,1)S(1)}, u32[]{:S(2)}, u32[]{:S(2)}) async-start(bf16[128,8,256]{2,1,0:T(8,128)(2,1)} %shard_map.81), calls=%async_computation.3 | async-start | bytes 1048576 | tf_op jit(solution)/shard_map/all_to_all | solution.py:350
  92.0 7.6 %collective-permute-start.4 = (f32[392,512]{1,0:T(8,128)}, f32[392,512]{1,0:T(8,128)S(1)}, u32[]{:S(2)}, u32[]{:S(2)}) collective-permute-start(f32[392,512]{1,0:T(8,128)} %copy-done.6), channel_id=1, source_target_pairs={{0,16},{16,0},{1,17},{17,1},{2,18},{18,2},{3,19},{19,3},{4,20},{20... | collective-permute-start | bytes 2408456 | tf_op jit(solution)/shard_map/ppermute | solution.py:317
  94.8 4.0 %collective-permute-start.3 = (bf16[256,1280]{1,0:T(8,128)(2,1)S(1)}, bf16[256,1280]{1,0:T(8,128)(2,1)S(1)}, u32[]{:S(2)}, u32[]{:S(2)}) collective-permute-start(bf16[256,1280]{1,0:T(8,128)(2,1)S(1)} %copy-done.3), channel_id=1, source_target_pairs={{0,16},{16,0},{1,17},{17,1},{2,18},{18,2},{3,19},{19,3},{4,20},{20... | collective-permute-start | bytes 1966088 | tf_op jit(solution)/shard_map/ppermute | solution.py:317
  98.8 0.8 copy-start.4
  111.4 1.1 copy-start.5

commit v4 on v3

--- a/solution.py
+++ b/solution.py
@@ -241,7 +241,9 @@
         out_ref[k * 8:(k + 1) * 8, :, LANES:2 * LANES] = high.reshape(8, 8, LANES).astype(BF)
 
 
-def last_kernel(got_ref, g_ref, g2_ref, keep_ref, keep2_ref, tg_ref, eg_ref, og_ref):
+def last_kernel(got_ref, g_ref, g2_hbm, keep_ref, keep2_ref, tg_ref, eg_ref, og_ref, g2_ref, sem):
+    fetch = pltpu.make_async_copy(g2_hbm, g2_ref, sem)
+    fetch.start()
     xl, y, core = lax.axis_index("xl"), lax.axis_index("y"), lax.axis_index("core")
     big = (8, 2, 8, 8, LANES)
     t0 = got_ref[:, :, 0:LANES].astype(F32).reshape(big)
@@ -291,6 +293,8 @@
         disp = kr[0:128, :] * alpha
         grad = kr[128:256, :] + disp * (kr[256:384, :] + shift)
         left = jnp.concatenate([grad.astype(BF), disp.astype(BF)], axis=0)
+        if h == 1:
+            fetch.wait()
         x = tn(left, gr[...])
         total_grad = x if h == 0 else total_grad + x
     tg_ref[...] = total_grad.astype(BF)
@@ -348,10 +352,15 @@
     g2, keep2 = swap(g), swap(send)
     op = call(x_kernel, shape(128, 8, 2 * LANES), got)
     got = lax.all_to_all(op, YZ, 0, 0, tiled=True)
-    return call(
+    vm = pl.BlockSpec(memory_space=pltpu.VMEM)
+    return pl.pallas_call(
         last_kernel,
-        [shape(512, 1280), shape(16, WIDE, dtype=f32), shape(16, WIDE, dtype=f32)],
-        got, g, g2, keep, keep2)
+        out_shape=[shape(512, 1280), shape(16, WIDE, dtype=f32), shape(16, WIDE, dtype=f32)],
+        in_specs=[vm, vm, pl.BlockSpec(memory_space=pl.ANY), vm, vm],
+        out_specs=[vm] * 3,
+        scratch_shapes=[pltpu.VMEM((256, 1280), BF), pltpu.SemaphoreType.DMA],
+        compiler_params=pltpu.CompilerParams(vmem_limit_bytes=VMEM_BYTES),
+    )(got, g, g2, keep, keep2)
 
 
 def solution(mesh):

time: 116 us -> 116 us (level)
    pallas_call x0 -> x1, Pallas kernels: none -> 3.21 us  [per_device(): pl.pallas_call(last_kernel, out_shape=[shape(512, 1280), shape(16, WIDE,...]
    pallas_call x6 -> x5, Pallas kernels: 7.95 us -> 5.42 us  [call(): pl.pallas_call(kernel, out_shape=outs, in_specs=[vm] * len(args), out_spe...]
where the time goes in v4:
time: 116 us
  blocking collectives  38.9 us (34%)
  starting transfers between devices  38.2 us (33%)
  waiting for transfers between devices  25.6 us (22%)
  Pallas kernels  10.2 us (9%)
  local copies, waits for them, and re-layouts  1.95 us (2%)
    all_to_all x2, blocking collectives, per_device(): got = lax.all_to_all(op, X, 0, 0, tiled=True)  38.9 us
    all_to_all x2, starting transfers between devices, per_device(): got = lax.all_to_all(op, YZ, 0, 0, tiled=True)  24.8 us
    all_to_all x2, waiting for transfers between devices, per_device(): got = lax.all_to_all(op, YZ, 0, 0, tiled=True)  23.5 us
    ppermute x5, starting transfers between devices, swap(): return lax.ppermute(x, 'core', [(0, 1), (1, 0)])  13.4 us
    pallas_call x5, Pallas kernels, call(): pl.pallas_call(kernel, out_shape=outs, in_specs=[vm] * len(args), out_spe...  5.42 us
    pallas_call x1, Pallas kernels, per_device(): pl.pallas_call(last_kernel, out_shape=[shape(512, 1280), shape(16, WIDE,...  3.21 us
  transfers between devices with their start and end apart: 7, of which 3 were waited for; matrix products, arithmetic and copies ran while one was open for 0% of the time, Pallas kernels for 1%

profile of v4, /device:TPU:1, one launch (start us, length us, event | category | flops | bytes accessed | tf_op | source)
XLA Modules:
  0.0 115.7 jit_solution(4160309088553915778)
XLA Ops:
  0.6 1.5 %shard_map.76 = bf16[128,8,128]{2,1,0:T(8,128)(2,1)} custom-call(bf16[16,40]{1,0:T(8,128)(2,1)} %e_ref.1, bf16[16,40]{1,0:T(8,128)(2,1)} %o_ref.1, bf16[16,40]{1,0:T(8,128)(2,1)} %i_ref.1), custom_call_target="tpu_custom_call" | custom-call | tf_op jit(solution)/shard_map/pallas_call | solution.py:326
  2.2 18.4 %all-to-all-start = ((bf16[128,8,128]{2,1,0:T(8,128)(2,1)}), bf16[128,8,128]{2,1,0:T(8,128)(2,1)S(1)}, u32[]{:S(2)}, u32[]{:S(2)}) async-start(bf16[128,8,128]{2,1,0:T(8,128)(2,1)} %shard_map.76), calls=%async_computation | async-start | bytes 524288 | tf_op jit(solution)/shard_map/all_to_all | solution.py:336
  20.6 0.0 copy-start
  20.6 2.9 %collective-permute-start = (bf16[512,1280]{1,0:T(8,128)(2,1)}, bf16[512,1280]{1,0:T(8,128)(2,1)S(1)}, u32[]{:S(2)}, u32[]{:S(2)}) collective-permute-start(bf16[512,1280]{1,0:T(8,128)(2,1)} %tok_ref.5), channel_id=1, source_target_pairs={{0,16},{16,0},{1,17},{17,1},{2,18},{18,2},{3,19},{19,3},{4,20},{20... | collective-permute-start | bytes 3932168 | tf_op jit(solution)/shard_map/ppermute | solution.py:321
  23.6 11.8 %all-to-all-done.got_ref = bf16[128,8,128]{2,1,0:T(8,128)(2,1)S(1)} async-done(((bf16[128,8,128]{2,1,0:T(8,128)(2,1)}), bf16[128,8,128]{2,1,0:T(8,128)(2,1)S(1)}, u32[]{:S(2)}, u32[]{:S(2)}) %all-to-all-start) | async-done | bytes 262176 | tf_op jit(solution)/shard_map/all_to_all | solution.py:336
  35.3 0.3 shard_map.77
  35.6 2.3 %collective-permute-start.1 = (bf16[512,1280]{1,0:T(8,128)(2,1)}, bf16[512,1280]{1,0:T(8,128)(2,1)S(1)}, u32[]{:S(2)}, u32[]{:S(2)}) collective-permute-start(bf16[512,1280]{1,0:T(8,128)(2,1)} %og_ref.3), channel_id=1, source_target_pairs={{0,16},{16,0},{1,17},{17,1},{2,18},{18,2},{3,19},{19,3},{4,20},{20... | collective-permute-start | bytes 3932168 | tf_op jit(solution)/shard_map/ppermute | solution.py:321
  37.9 17.6 %all_to_all.20.got_ref = bf16[4,192,640]{2,1,0:T(8,128)(2,1)S(1)} all-to-all(bf16[4,192,640]{2,1,0:T(8,128)(2,1)S(1)} %shard_map.77), channel_id=1, replica_groups=mesh['xh'=2,'z'=8,'core'=2,'y'=8,'xl'=2] {'xh','xl'}, dimensions={0} | all-to-all | bytes 1966080 | tf_op jit(solution)/shard_map/all_to_all | solution.py:340
  55.6 0.0 collective-permute-done.tok2_ref
  55.6 0.0 collective-permute-done.1.og2_ref
  55.6 0.0 copy-done
  55.6 0.0 copy-done.1
  55.6 1.7 %shard_map.78 = (bf16[256,1280]{1,0:T(8,128)(2,1)S(1)}, f32[128,1024]{1,0:T(8,128)S(1)}, f32[128,1024]{1,0:T(8,128)S(1)}, f32[128,1024]{1,0:T(8,128)S(1)}, f32[8,1024]{1,0:T(8,128)S(1)}) custom-call(bf16[4,192,640]{2,1,0:T(8,128)(2,1)S(1)} %all_to_all.20.got_ref, bf16[512,1280]{1,0:T(8,128)(2,1)S(1)} %copy-done, ...), custom_call_target="tpu_custom_call" | custom-call | tf_op jit(solution)/shard_map/pallas_call | solution.py:306
  57.3 0.0 copy-start.2
  57.3 3.4 %collective-permute-start.2 = (f32[8,1024]{1,0:T(8,128)S(1)}, f32[8,1024]{1,0:T(8,128)S(1)}, u32[]{:S(2)}, u32[]{:S(2)}) collective-permute-start(f32[8,1024]{1,0:T(8,128)S(1)} %get-tuple-element.25.r_ref), channel_id=1, source_target_pairs={{0,16},{16,0},{1,17},{17,1},{2,18},{18,2},{3,19},{19,3},{4,20},{20... | collective-permute-start | bytes 98312 | tf_op jit(solution)/shard_map/ppermute | solution.py:321
  60.7 1.1 shard_map.79
  61.8 0.0 copy-done.2
  61.8 0.0 collective-permute-done.2.r2_ref
  61.9 1.0 shard_map.80
  62.8 0.0 copy-start.6
  62.8 21.3 %all_to_all.21.got_ref = bf16[4,272,640]{2,1,0:T(8,128)(2,1)S(1)} all-to-all(bf16[4,272,640]{2,1,0:T(8,128)(2,1)S(1)} %get-tuple-element.31), channel_id=1, replica_groups=mesh['xh'=2,'z'=8,'core'=2,'y'=8,'xl'=2] {'xh','xl'}, dimensions={0} | all-to-all | bytes 2785280 | tf_op jit(solution)/shard_map/all_to_all | solution.py:351
  84.1 0.0 copy-done.6
  84.1 1.4 %shard_map.81 = bf16[128,8,256]{2,1,0:T(8,128)(2,1)} custom-call(bf16[4,272,640]{2,1,0:T(8,128)(2,1)S(1)} %all_to_all.21.got_ref), custom_call_target="tpu_custom_call" | custom-call | tf_op jit(solution)/shard_map/pallas_call | solution.py:306
  85.6 6.4 %all-to-all-start.3 = ((bf16[128,8,256]{2,1,0:T(8,128)(2,1)}), bf16[128,8,256]{2,1,0:T(8,128)(2,1)S(1)}, u32[]{:S(2)}, u32[]{:S(2)}) async-start(bf16[128,8,256]{2,1,0:T(8,128)(2,1)} %shard_map.81), calls=%async_computation.3 | async-start | bytes 1048576 | tf_op jit(solution)/shard_map/all_to_all | solution.py:354
  92.0 2.8 %collective-permute-start.4 = (f32[392,512]{1,0:T(8,128)}, f32[392,512]{1,0:T(8,128)S(1)}, u32[]{:S(2)}, u32[]{:S(2)}) collective-permute-start(f32[392,512]{1,0:T(8,128)} %copy-done.6), channel_id=1, source_target_pairs={{0,16},{16,0},{1,17},{17,1},{2,18},{18,2},{3,19},{19,3},{4,20},{20... | collective-permute-start | bytes 2408456 | tf_op jit(solution)/shard_map/ppermute | solution.py:321
  94.8 1.9 %collective-permute-start.3 = (bf16[256,1280]{1,0:T(8,128)(2,1)S(1)}, bf16[256,1280]{1,0:T(8,128)(2,1)S(1)}, u32[]{:S(2)}, u32[]{:S(2)}) collective-permute-start(bf16[256,1280]{1,0:T(8,128)(2,1)S(1)} %copy-done.3), channel_id=1, source_target_pairs={{0,16},{16,0},{1,17},{17,1},{2,18},{18,2},{3,19},{19,3},{4,20},{20... | collective-permute-start | bytes 1966088 | tf_op jit(solution)/shard_map/ppermute | solution.py:321
  96.7 2.1 %collective-permute-done.3.g2_hbm = bf16[256,1280]{1,0:T(8,128)(2,1)S(1)} collective-permute-done((bf16[256,1280]{1,0:T(8,128)(2,1)S(1)}, bf16[256,1280]{1,0:T(8,128)(2,1)S(1)}, u32[]{:S(2)}, u32[]{:S(2)}) %collective-permute-start.3) | collective-permute-done | bytes 655392 | tf_op jit(solution)/shard_map/ppermute | solution.py:321
  98.8 0.8 copy-done.4
  99.6 0.0 collective-permute-done.4.keep2_ref
  99.6 11.8 %all-to-all-done.3.got_ref = bf16[128,8,256]{2,1,0:T(8,128)(2,1)S(1)} async-done(((bf16[128,8,256]{2,1,0:T(8,128)(2,1)}), bf16[128,8,256]{2,1,0:T(8,128)(2,1)S(1)}, u32[]{:S(2)}, u32[]{:S(2)}) %all-to-all-start.3) | async-done | bytes 524320 | tf_op jit(solution)/shard_map/all_to_all | solution.py:354
  111.4 1.1 copy-done.5
  112.5 3.2 %shard_map.82 = (bf16[512,1280]{1,0:T(8,128)(2,1)}, f32[16,40]{1,0:T(8,128)}, f32[16,40]{1,0:T(8,128)}) custom-call(bf16[128,8,256]{2,1,0:T(8,128)(2,1)S(1)} %all-to-all-done.3.got_ref, bf16[256,1280]{1,0:T(8,128)(2,1)S(1)} %copy-done.3, bf16[256,1280]{1,0:T(8,128)(2,1)S(1)} %copy-done.5, f32[392,512]{1,0:T(8,128)S(1)} %get-tuple-element.33.keep_ref, ...), custom_call_target="tpu_custom_call" | custom-call | tf_op jit(solution)/shard_map/pallas_call | solution.py:356
  (5 shorter events, 0.0 us)
Async XLA Ops:
  2.2 33.2 %all-to-all-start = ((bf16[128,8,128]{2,1,0:T(8,128)(2,1)}), bf16[128,8,128]{2,1,0:T(8,128)(2,1)S(1)}, u32[]{:S(2)}, u32[]{:S(2)}) async-start(bf16[128,8,128]{2,1,0:T(8,128)(2,1)} %shard_map.76), calls=%async_computation | async-start | bytes 524288 | tf_op jit(solution)/shard_map/all_to_all | solution.py:336
  20.6 35.0 %copy-start = (bf16[512,1280]{1,0:T(8,128)(2,1)S(1)}, bf16[512,1280]{1,0:T(8,128)(2,1)}, u32[]{:S(2)}) copy-start(bf16[512,1280]{1,0:T(8,128)(2,1)} %tok_ref.5) | copy-start | bytes 3932164
  20.6 34.9 %collective-permute-start = (bf16[512,1280]{1,0:T(8,128)(2,1)}, bf16[512,1280]{1,0:T(8,128)(2,1)S(1)}, u32[]{:S(2)}, u32[]{:S(2)}) collective-permute-start(bf16[512,1280]{1,0:T(8,128)(2,1)} %tok_ref.5), channel_id=1, source_target_pairs={{0,16},{16,0},{1,17},{17,1},{2,18},{18,2},{3,19},{19,3},{4,20},{20... | collective-permute-start | bytes 3932168 | tf_op jit(solution)/shard_map/ppermute | solution.py:321
  35.3 20.2 %copy-start.1 = (bf16[512,1280]{1,0:T(8,128)(2,1)S(1)}, bf16[512,1280]{1,0:T(8,128)(2,1)}, u32[]{:S(2)}) copy-start(bf16[512,1280]{1,0:T(8,128)(2,1)} %og_ref.3) | copy-start | bytes 3932164
  35.6 20.0 %collective-permute-start.1 = (bf16[512,1280]{1,0:T(8,128)(2,1)}, bf16[512,1280]{1,0:T(8,128)(2,1)S(1)}, u32[]{:S(2)}, u32[]{:S(2)}) collective-permute-start(bf16[512,1280]{1,0:T(8,128)(2,1)} %og_ref.3), channel_id=1, source_target_pairs={{0,16},{16,0},{1,17},{17,1},{2,18},{18,2},{3,19},{19,3},{4,20},{20... | collective-permute-start | bytes 3932168 | tf_op jit(solution)/shard_map/ppermute | solution.py:321
  57.3 4.5 %copy-start.2 = (bf16[256,1280]{1,0:T(8,128)(2,1)}, bf16[256,1280]{1,0:T(8,128)(2,1)S(1)}, u32[]{:S(2)}) copy-start(bf16[256,1280]{1,0:T(8,128)(2,1)S(1)} %get-tuple-element.32.g_ref) | copy-start | bytes 1966084
  57.3 4.5 %collective-permute-start.2 = (f32[8,1024]{1,0:T(8,128)S(1)}, f32[8,1024]{1,0:T(8,128)S(1)}, u32[]{:S(2)}, u32[]{:S(2)}) collective-permute-start(f32[8,1024]{1,0:T(8,128)S(1)} %get-tuple-element.25.r_ref), channel_id=1, source_target_pairs={{0,16},{16,0},{1,17},{17,1},{2,18},{18,2},{3,19},{19,3},{4,20},{20... | collective-permute-start | bytes 98312 | tf_op jit(solution)/shard_map/ppermute | solution.py:321
  62.8 21.3 %copy-start.6 = (f32[392,512]{1,0:T(8,128)}, f32[392,512]{1,0:T(8,128)S(1)}, u32[]{:S(2)}) copy-start(f32[392,512]{1,0:T(8,128)S(1)} %get-tuple-element.34) | copy-start | bytes 2408452
  84.1 10.6 %copy-start.3 = (bf16[256,1280]{1,0:T(8,128)(2,1)S(1)}, bf16[256,1280]{1,0:T(8,128)(2,1)}, u32[]{:S(2)}) copy-start(bf16[256,1280]{1,0:T(8,128)(2,1)} %copy-done.2) | copy-start | bytes 1966084
  85.6 25.8 %all-to-all-start.3 = ((bf16[128,8,256]{2,1,0:T(8,128)(2,1)}), bf16[128,8,256]{2,1,0:T(8,128)(2,1)S(1)}, u32[]{:S(2)}, u32[]{:S(2)}) async-start(bf16[128,8,256]{2,1,0:T(8,128)(2,1)} %shard_map.81), calls=%async_computation.3 | async-start | bytes 1048576 | tf_op jit(solution)/shard_map/all_to_all | solution.py:354
  92.0 7.6 %collective-permute-start.4 = (f32[392,512]{1,0:T(8,128)}, f32[392,512]{1,0:T(8,128)S(1)}, u32[]{:S(2)}, u32[]{:S(2)}) collective-permute-start(f32[392,512]{1,0:T(8,128)} %copy-done.6), channel_id=1, source_target_pairs={{0,16},{16,0},{1,17},{17,1},{2,18},{18,2},{3,19},{19,3},{4,20},{20... | collective-permute-start | bytes 2408456 | tf_op jit(solution)/shard_map/ppermute | solution.py:321
  94.8 4.0 %collective-permute-start.3 = (bf16[256,1280]{1,0:T(8,128)(2,1)S(1)}, bf16[256,1280]{1,0:T(8,128)(2,1)S(1)}, u32[]{:S(2)}, u32[]{:S(2)}) collective-permute-start(bf16[256,1280]{1,0:T(8,128)(2,1)S(1)} %copy-done.3), channel_id=1, source_target_pairs={{0,16},{16,0},{1,17},{17,1},{2,18},{18,2},{3,19},{19,3},{4,20},{20... | collective-permute-start | bytes 1966088 | tf_op jit(solution)/shard_map/ppermute | solution.py:321
  98.8 0.8 copy-start.4
  111.4 1.1 copy-start.5

commit v5 on v3

--- a/solution.py
+++ b/solution.py
@@ -62,7 +62,7 @@
     a, b, c = split(p, 3)
     rest = jnp.zeros((8, 640 - 3 * LANES), BF)
     top = jnp.concatenate([a, b, c, rest], axis=1).astype(F32)
-    return jnp.concatenate([top, jnp.zeros((8, 640), F32)], axis=0).astype(BF)
+    return top.astype(BF)
 
 
 def stat_read(rows):
@@ -179,7 +179,7 @@
     put(3, bc_ref[128:256, :])
     stats = stat_rows(p_ref[...])
     for j in range(4):
-        out_ref[j, 256:272, :] = stats
+        out_ref[j, 256:264, :] = stats
 
 
 def merge_stats(ps, groups, exact=True):
@@ -206,7 +206,7 @@
 
 def x_kernel(got_ref, out_ref):
     xl = lax.axis_index("xl")
-    top, total, mean, ws, ds = merge_stats([stat_read(got_ref[j, 256:272, :]) for j in range(4)], 16, False)
+    top, total, mean, ws, ds = merge_stats([stat_read(got_ref[j, 256:264, :]) for j in range(4)], 16, False)
     ws = [columns(w, 8, xl * 8) for w in ws]
     ds = [columns(d, 8, xl * 8) for d in ds]
 
@@ -342,7 +342,7 @@
     e, dc, p, bc = call(
         slots_kernel, [wide, wide, shape(8, LANES, dtype=f32), shape(256, 1280)], lg, dg, tokens, tok2)
     op, keep, send = call(
-        tokens_kernel, [shape(4, 272, 640), shape(392, 512, dtype=f32), shape(392, 512, dtype=f32)],
+        tokens_kernel, [shape(4, 264, 640), shape(392, 512, dtype=f32), shape(392, 512, dtype=f32)],
         lg, cg, r, r2, e, dc, p, bc, tokens, tok2, output_grad, og2)
     got = lax.all_to_all(op, X, 0, 0, tiled=True)
     g2, keep2 = swap(g), swap(send)

time: 116 us -> 115 us (level)
  no operation moved by 1% of the time
where the time goes in v5:
time: 115 us
  blocking collectives  38.5 us (33%)
  starting transfers between devices  38.2 us (33%)
  waiting for transfers between devices  25.6 us (22%)
  Pallas kernels  9.49 us (8%)
  local copies, waits for them, and re-layouts  1.95 us (2%)
    all_to_all x2, blocking collectives, per_device(): got = lax.all_to_all(op, X, 0, 0, tiled=True)  38.5 us
    all_to_all x2, starting transfers between devices, per_device(): got = lax.all_to_all(op, YZ, 0, 0, tiled=True)  24.8 us
    all_to_all x2, waiting for transfers between devices, per_device(): got = lax.all_to_all(op, YZ, 0, 0, tiled=True)  23.5 us
    ppermute x5, starting transfers between devices, swap(): return lax.ppermute(x, 'core', [(0, 1), (1, 0)])  13.4 us
    pallas_call x6, Pallas kernels, call(): pl.pallas_call(kernel, out_shape=outs, in_specs=[vm] * len(args), out_spe...  7.95 us
  transfers between devices with their start and end apart: 7, of which 3 were waited for; matrix products, arithmetic and copies ran while one was open for 0% of the time, Pallas kernels for 1%

profile of v5, /device:TPU:1, one launch (start us, length us, event | category | flops | bytes accessed | tf_op | source)
XLA Modules:
  0.0 114.5 jit_solution(4408840968034720959)
XLA Ops:
  0.6 1.5 %shard_map.76 = bf16[128,8,128]{2,1,0:T(8,128)(2,1)} custom-call(bf16[16,40]{1,0:T(8,128)(2,1)} %e_ref.1, bf16[16,40]{1,0:T(8,128)(2,1)} %o_ref.1, bf16[16,40]{1,0:T(8,128)(2,1)} %i_ref.1), custom_call_target="tpu_custom_call" | custom-call | tf_op jit(solution)/shard_map/pallas_call | solution.py:322
  2.2 18.4 %all-to-all-start = ((bf16[128,8,128]{2,1,0:T(8,128)(2,1)}), bf16[128,8,128]{2,1,0:T(8,128)(2,1)S(1)}, u32[]{:S(2)}, u32[]{:S(2)}) async-start(bf16[128,8,128]{2,1,0:T(8,128)(2,1)} %shard_map.76), calls=%async_computation | async-start | bytes 524288 | tf_op jit(solution)/shard_map/all_to_all | solution.py:332
  20.6 0.0 copy-start
  20.6 2.9 %collective-permute-start = (bf16[512,1280]{1,0:T(8,128)(2,1)}, bf16[512,1280]{1,0:T(8,128)(2,1)S(1)}, u32[]{:S(2)}, u32[]{:S(2)}) collective-permute-start(bf16[512,1280]{1,0:T(8,128)(2,1)} %tok_ref.5), channel_id=1, source_target_pairs={{0,16},{16,0},{1,17},{17,1},{2,18},{18,2},{3,19},{19,3},{4,20},{20... | collective-permute-start | bytes 3932168 | tf_op jit(solution)/shard_map/ppermute | solution.py:317
  23.6 11.8 %all-to-all-done.got_ref = bf16[128,8,128]{2,1,0:T(8,128)(2,1)S(1)} async-done(((bf16[128,8,128]{2,1,0:T(8,128)(2,1)}), bf16[128,8,128]{2,1,0:T(8,128)(2,1)S(1)}, u32[]{:S(2)}, u32[]{:S(2)}) %all-to-all-start) | async-done | bytes 262176 | tf_op jit(solution)/shard_map/all_to_all | solution.py:332
  35.3 0.3 shard_map.77
  35.6 2.3 %collective-permute-start.1 = (bf16[512,1280]{1,0:T(8,128)(2,1)}, bf16[512,1280]{1,0:T(8,128)(2,1)S(1)}, u32[]{:S(2)}, u32[]{:S(2)}) collective-permute-start(bf16[512,1280]{1,0:T(8,128)(2,1)} %og_ref.3), channel_id=1, source_target_pairs={{0,16},{16,0},{1,17},{17,1},{2,18},{18,2},{3,19},{19,3},{4,20},{20... | collective-permute-start | bytes 3932168 | tf_op jit(solution)/shard_map/ppermute | solution.py:317
  37.9 17.6 %all_to_all.20.got_ref = bf16[4,192,640]{2,1,0:T(8,128)(2,1)S(1)} all-to-all(bf16[4,192,640]{2,1,0:T(8,128)(2,1)S(1)} %shard_map.77), channel_id=1, replica_groups=mesh['xh'=2,'z'=8,'core'=2,'y'=8,'xl'=2] {'xh','xl'}, dimensions={0} | all-to-all | bytes 1966080 | tf_op jit(solution)/shard_map/all_to_all | solution.py:336
  55.6 0.0 collective-permute-done.tok2_ref
  55.6 0.0 collective-permute-done.1.og2_ref
  55.6 0.0 copy-done
  55.6 0.0 copy-done.1
  55.6 1.7 %shard_map.78 = (bf16[256,1280]{1,0:T(8,128)(2,1)S(1)}, f32[128,1024]{1,0:T(8,128)S(1)}, f32[128,1024]{1,0:T(8,128)S(1)}, f32[128,1024]{1,0:T(8,128)S(1)}, f32[8,1024]{1,0:T(8,128)S(1)}) custom-call(bf16[4,192,640]{2,1,0:T(8,128)(2,1)S(1)} %all_to_all.20.got_ref, bf16[512,1280]{1,0:T(8,128)(2,1)S(1)} %copy-done, ...), custom_call_target="tpu_custom_call" | custom-call | tf_op jit(solution)/shard_map/pallas_call | solution.py:302
  57.3 0.0 copy-start.2
  57.3 3.4 %collective-permute-start.2 = (f32[8,1024]{1,0:T(8,128)S(1)}, f32[8,1024]{1,0:T(8,128)S(1)}, u32[]{:S(2)}, u32[]{:S(2)}) collective-permute-start(f32[8,1024]{1,0:T(8,128)S(1)} %get-tuple-element.25.r_ref), channel_id=1, source_target_pairs={{0,16},{16,0},{1,17},{17,1},{2,18},{18,2},{3,19},{19,3},{4,20},{20... | collective-permute-start | bytes 98312 | tf_op jit(solution)/shard_map/ppermute | solution.py:317
  60.7 1.1 shard_map.79
  61.8 0.0 copy-done.2
  61.8 0.0 collective-permute-done.2.r2_ref
  61.9 1.0 shard_map.80
  62.8 0.0 copy-start.6
  62.8 20.8 %all_to_all.21.got_ref = bf16[4,264,640]{2,1,0:T(8,128)(2,1)S(1)} all-to-all(bf16[4,264,640]{2,1,0:T(8,128)(2,1)S(1)} %get-tuple-element.31), channel_id=1, replica_groups=mesh['xh'=2,'z'=8,'core'=2,'y'=8,'xl'=2] {'xh','xl'}, dimensions={0} | all-to-all | bytes 2703360 | tf_op jit(solution)/shard_map/all_to_all | solution.py:347
  83.7 0.0 copy-done.6
  83.7 1.4 %shard_map.81 = bf16[128,8,256]{2,1,0:T(8,128)(2,1)} custom-call(bf16[4,264,640]{2,1,0:T(8,128)(2,1)S(1)} %all_to_all.21.got_ref), custom_call_target="tpu_custom_call" | custom-call | tf_op jit(solution)/shard_map/pallas_call | solution.py:302
  85.1 6.4 %all-to-all-start.3 = ((bf16[128,8,256]{2,1,0:T(8,128)(2,1)}), bf16[128,8,256]{2,1,0:T(8,128)(2,1)S(1)}, u32[]{:S(2)}, u32[]{:S(2)}) async-start(bf16[128,8,256]{2,1,0:T(8,128)(2,1)} %shard_map.81), calls=%async_computation.3 | async-start | bytes 1048576 | tf_op jit(solution)/shard_map/all_to_all | solution.py:350
  91.5 2.8 %collective-permute-start.4 = (f32[392,512]{1,0:T(8,128)}, f32[392,512]{1,0:T(8,128)S(1)}, u32[]{:S(2)}, u32[]{:S(2)}) collective-permute-start(f32[392,512]{1,0:T(8,128)} %copy-done.6), channel_id=1, source_target_pairs={{0,16},{16,0},{1,17},{17,1},{2,18},{18,2},{3,19},{19,3},{4,20},{20... | collective-permute-start | bytes 2408456 | tf_op jit(solution)/shard_map/ppermute | solution.py:317
  94.3 1.9 %collective-permute-start.3 = (bf16[256,1280]{1,0:T(8,128)(2,1)S(1)}, bf16[256,1280]{1,0:T(8,128)(2,1)S(1)}, u32[]{:S(2)}, u32[]{:S(2)}) collective-permute-start(bf16[256,1280]{1,0:T(8,128)(2,1)S(1)} %copy-done.3), channel_id=1, source_target_pairs={{0,16},{16,0},{1,17},{17,1},{2,18},{18,2},{3,19},{19,3},{4,20},{20... | collective-permute-start | bytes 1966088 | tf_op jit(solution)/shard_map/ppermute | solution.py:317
  96.2 2.1 %collective-permute-done.3.g2_ref = bf16[256,1280]{1,0:T(8,128)(2,1)S(1)} collective-permute-done((bf16[256,1280]{1,0:T(8,128)(2,1)S(1)}, bf16[256,1280]{1,0:T(8,128)(2,1)S(1)}, u32[]{:S(2)}, u32[]{:S(2)}) %collective-permute-start.3) | collective-permute-done | bytes 655392 | tf_op jit(solution)/shard_map/ppermute | solution.py:317
  98.3 0.8 copy-done.4
  99.1 0.0 collective-permute-done.4.keep2_ref
  99.2 11.8 %all-to-all-done.3.got_ref = bf16[128,8,256]{2,1,0:T(8,128)(2,1)S(1)} async-done(((bf16[128,8,256]{2,1,0:T(8,128)(2,1)}), bf16[128,8,256]{2,1,0:T(8,128)(2,1)S(1)}, u32[]{:S(2)}, u32[]{:S(2)}) %all-to-all-start.3) | async-done | bytes 524320 | tf_op jit(solution)/shard_map/all_to_all | solution.py:350
  110.9 1.1 copy-done.5
  112.0 2.5 %shard_map.82 = (bf16[512,1280]{1,0:T(8,128)(2,1)}, f32[16,40]{1,0:T(8,128)}, f32[16,40]{1,0:T(8,128)}) custom-call(bf16[128,8,256]{2,1,0:T(8,128)(2,1)S(1)} %all-to-all-done.3.got_ref, bf16[256,1280]{1,0:T(8,128)(2,1)S(1)} %copy-done.3, bf16[256,1280]{1,0:T(8,128)(2,1)S(1)} %copy-done.5, f32[392,512]{1,0:T(8,128)S(1)} %get-tuple-element.33.keep_ref, ...), custom_call_target="tpu_custom_call" | custom-call | tf_op jit(solution)/shard_map/pallas_call | solution.py:302
  (5 shorter events, 0.0 us)
Async XLA Ops:
  2.2 33.2 %all-to-all-start = ((bf16[128,8,128]{2,1,0:T(8,128)(2,1)}), bf16[128,8,128]{2,1,0:T(8,128)(2,1)S(1)}, u32[]{:S(2)}, u32[]{:S(2)}) async-start(bf16[128,8,128]{2,1,0:T(8,128)(2,1)} %shard_map.76), calls=%async_computation | async-start | bytes 524288 | tf_op jit(solution)/shard_map/all_to_all | solution.py:332
  20.6 35.0 %copy-start = (bf16[512,1280]{1,0:T(8,128)(2,1)S(1)}, bf16[512,1280]{1,0:T(8,128)(2,1)}, u32[]{:S(2)}) copy-start(bf16[512,1280]{1,0:T(8,128)(2,1)} %tok_ref.5) | copy-start | bytes 3932164
  20.6 34.9 %collective-permute-start = (bf16[512,1280]{1,0:T(8,128)(2,1)}, bf16[512,1280]{1,0:T(8,128)(2,1)S(1)}, u32[]{:S(2)}, u32[]{:S(2)}) collective-permute-start(bf16[512,1280]{1,0:T(8,128)(2,1)} %tok_ref.5), channel_id=1, source_target_pairs={{0,16},{16,0},{1,17},{17,1},{2,18},{18,2},{3,19},{19,3},{4,20},{20... | collective-permute-start | bytes 3932168 | tf_op jit(solution)/shard_map/ppermute | solution.py:317
  35.3 20.2 %copy-start.1 = (bf16[512,1280]{1,0:T(8,128)(2,1)S(1)}, bf16[512,1280]{1,0:T(8,128)(2,1)}, u32[]{:S(2)}) copy-start(bf16[512,1280]{1,0:T(8,128)(2,1)} %og_ref.3) | copy-start | bytes 3932164
  35.6 20.0 %collective-permute-start.1 = (bf16[512,1280]{1,0:T(8,128)(2,1)}, bf16[512,1280]{1,0:T(8,128)(2,1)S(1)}, u32[]{:S(2)}, u32[]{:S(2)}) collective-permute-start(bf16[512,1280]{1,0:T(8,128)(2,1)} %og_ref.3), channel_id=1, source_target_pairs={{0,16},{16,0},{1,17},{17,1},{2,18},{18,2},{3,19},{19,3},{4,20},{20... | collective-permute-start | bytes 3932168 | tf_op jit(solution)/shard_map/ppermute | solution.py:317
  57.3 4.5 %copy-start.2 = (bf16[256,1280]{1,0:T(8,128)(2,1)}, bf16[256,1280]{1,0:T(8,128)(2,1)S(1)}, u32[]{:S(2)}) copy-start(bf16[256,1280]{1,0:T(8,128)(2,1)S(1)} %get-tuple-element.32.g_ref) | copy-start | bytes 1966084
  57.3 4.5 %collective-permute-start.2 = (f32[8,1024]{1,0:T(8,128)S(1)}, f32[8,1024]{1,0:T(8,128)S(1)}, u32[]{:S(2)}, u32[]{:S(2)}) collective-permute-start(f32[8,1024]{1,0:T(8,128)S(1)} %get-tuple-element.25.r_ref), channel_id=1, source_target_pairs={{0,16},{16,0},{1,17},{17,1},{2,18},{18,2},{3,19},{19,3},{4,20},{20... | collective-permute-start | bytes 98312 | tf_op jit(solution)/shard_map/ppermute | solution.py:317
  62.8 20.9 %copy-start.6 = (f32[392,512]{1,0:T(8,128)}, f32[392,512]{1,0:T(8,128)S(1)}, u32[]{:S(2)}) copy-start(f32[392,512]{1,0:T(8,128)S(1)} %get-tuple-element.34) | copy-start | bytes 2408452
  83.7 10.6 %copy-start.3 = (bf16[256,1280]{1,0:T(8,128)(2,1)S(1)}, bf16[256,1280]{1,0:T(8,128)(2,1)}, u32[]{:S(2)}) copy-start(bf16[256,1280]{1,0:T(8,128)(2,1)} %copy-done.2) | copy-start | bytes 1966084
  85.1 25.8 %all-to-all-start.3 = ((bf16[128,8,256]{2,1,0:T(8,128)(2,1)}), bf16[128,8,256]{2,1,0:T(8,128)(2,1)S(1)}, u32[]{:S(2)}, u32[]{:S(2)}) async-start(bf16[128,8,256]{2,1,0:T(8,128)(2,1)} %shard_map.81), calls=%async_computation.3 | async-start | bytes 1048576 | tf_op jit(solution)/shard_map/all_to_all | solution.py:350
  91.5 7.6 %collective-permute-start.4 = (f32[392,512]{1,0:T(8,128)}, f32[392,512]{1,0:T(8,128)S(1)}, u32[]{:S(2)}, u32[]{:S(2)}) collective-permute-start(f32[392,512]{1,0:T(8,128)} %copy-done.6), channel_id=1, source_target_pairs={{0,16},{16,0},{1,17},{17,1},{2,18},{18,2},{3,19},{19,3},{4,20},{20... | collective-permute-start | bytes 2408456 | tf_op jit(solution)/shard_map/ppermute | solution.py:317
  94.3 4.0 %collective-permute-start.3 = (bf16[256,1280]{1,0:T(8,128)(2,1)S(1)}, bf16[256,1280]{1,0:T(8,128)(2,1)S(1)}, u32[]{:S(2)}, u32[]{:S(2)}) collective-permute-start(bf16[256,1280]{1,0:T(8,128)(2,1)S(1)} %copy-done.3), channel_id=1, source_target_pairs={{0,16},{16,0},{1,17},{17,1},{2,18},{18,2},{3,19},{19,3},{4,20},{20... | collective-permute-start | bytes 1966088 | tf_op jit(solution)/shard_map/ppermute | solution.py:317
  98.3 0.8 copy-start.4
  110.9 1.1 copy-start.5
